TPU v7x, 256 devices: a whole 4x4x8 slice. The times are simulated.
256 devices in a mesh: gz: 8 (over x, core), row: 8 (over z), col: 4 (over y).
Axes of the slice: x: 4, y: 4, z: 8, core: 2. Of those that a mesh axis runs over, the one named last changes fastest.
Arguments:
- subtree_lower: bfloat16 [8, 4096, 2048], P('gz', 'row', 'col'), may hold values from -6 to 6
- subtree_upper: bfloat16 [8, 2048, 4096], P('gz', 'col', 'row'), may hold values from -0.125 to 0.125
- touched: int32 [8, 32], P('gz'), may hold values 0 or 1
- front: float32 [4096, 8, 4, 128], P('row', 'gz', 'col'), may hold values from -6 to 96
Outputs:
- lower_panel: float32 [4096, 128], P('row')
- upper_panel: float32 [128, 8, 4, 128], P(None, 'gz', 'col')
- trailing: float32 [4096, 8, 4, 128], P('row', 'gz', 'col')
All inputs are finite; a program needn't handle non-finite values. No bound on the sum of `touched` on one device may be relied on, other than what follows from the above.
Results may differ from a plain program's by a relative error of at most 0.0003.
Values may be sent and summed in bfloat16 or wider, within the bound.
A program may use at most 64 MiB of HBM per device.

v0:
```python
import jax
import jax.numpy as jnp
from jax import lax
from jax.experimental import pallas as pl
from jax.experimental.pallas import tpu as pltpu
from jax.sharding import PartitionSpec as P

BLOCK = 128


def exact_dot(left, right):
    return jnp.dot(
        left, right, precision=lax.Precision.HIGHEST, preferred_element_type=jnp.float32
    )


def eliminate(first, count, worked, product, lower, lower_inverse):
    rows = lax.broadcasted_iota(jnp.int32, (BLOCK, BLOCK), 0)
    lanes = lax.broadcasted_iota(jnp.int32, (BLOCK, BLOCK), 1)

    def step(at, carry):
        dense = worked[...]
        pivot_row = worked[pl.ds(at, 1), :]
        product_row = product[pl.ds(at, 1), :]
        lower_inverse[pl.ds(at, 1), :] = product_row
        column = jnp.sum(jnp.where(lanes == at, dense, 0.0), axis=1, keepdims=True)
        pivot = jnp.sum(
            jnp.where(lanes[:1] == at, pivot_row, 0.0), axis=1, keepdims=True
        )
        scaled = jnp.where(rows == at, 0.0, column / pivot)
        worked[...] = dense - scaled * pivot_row
        product[...] = product[...] - scaled * product_row
        lower[...] = jnp.where((lanes == at) & (rows > at), scaled, lower[...])
        return carry

    lax.fori_loop(first, first + count, step, 0)


def start_elimination(pivot, worked, product, lower):
    rows = lax.broadcasted_iota(jnp.int32, (BLOCK, BLOCK), 0)
    lanes = lax.broadcasted_iota(jnp.int32, (BLOCK, BLOCK), 1)
    identity = jnp.where(rows == lanes, 1.0, 0.0)
    worked[...] = pivot
    product[...] = identity
    lower[...] = identity


def finish_elimination(worked, product, lower):
    rows = lax.broadcasted_iota(jnp.int32, (BLOCK, BLOCK), 0)
    lanes = lax.broadcasted_iota(jnp.int32, (BLOCK, BLOCK), 1)
    pivots = jnp.sum(jnp.where(rows == lanes, worked[...], 0.0), axis=1, keepdims=True)
    return exact_dot(product[...] / pivots, lower[...])


def factor_kernel(pivot, lower_inverse, upper_inverse, worked, product, lower):
    start_elimination(pivot[...], worked, product, lower)
    eliminate(0, BLOCK, worked, product, lower, lower_inverse)
    upper_inverse[...] = finish_elimination(worked, product, lower)


def factor(pivot):
    square = jax.ShapeDtypeStruct((BLOCK, BLOCK), jnp.float32)
    return pl.pallas_call(
        factor_kernel,
        out_shape=(square, square),
        scratch_shapes=[pltpu.VMEM((BLOCK, BLOCK), jnp.float32)] * 3,
    )(pivot)


def broadcast(shard, axis, root):
    mine = lax.axis_index(axis) == root
    return lax.psum(jnp.where(mine, shard, jnp.zeros_like(shard)), axis)


def shards(subtree_lower, subtree_upper, touched, front):
    local_rows = front.shape[0]
    width = front.shape[3]
    marks = touched[0].astype(jnp.bfloat16)
    own_marks = lax.dynamic_slice_in_dim(
        marks, lax.axis_index("row") * (local_rows // width), local_rows // width
    )
    own_marks = jnp.repeat(own_marks, width)
    lower_kept = subtree_lower[0] * own_marks[:, None]
    upper_kept = subtree_upper[0] * own_marks[None, :]
    first = (
        (lax.axis_index("gz") == 0) & (lax.axis_index("row") == 0) & (lax.axis_index("col") == 0)
    )
    pivot_term = -jnp.dot(
        lower_kept[:width], upper_kept[:, :width], preferred_element_type=jnp.float32
    )
    pivot_term = jnp.where(lax.axis_index("row") == 0, pivot_term, 0.0)
    pivot_term = pivot_term + jnp.where(first, front[:width, 0, 0, :], 0.0)
    lower_inverse, upper_inverse = factor(lax.psum(pivot_term, ("gz", "row", "col")))
    layer_term = jnp.dot(
        lower_kept,
        lax.all_gather(upper_kept, "row", axis=1, tiled=True),
        preferred_element_type=jnp.float32,
    )
    blocks = layer_term.reshape(local_rows, 32, width).transpose(1, 0, 2)
    schur = lax.psum_scatter(blocks, ("gz", "col"), scatter_dimension=0, tiled=False)
    updated = front[:, 0, 0, :] - schur
    lower_panel = broadcast(exact_dot(updated, upper_inverse), ("gz", "col"), 0)
    upper_panel = broadcast(exact_dot(lower_inverse, updated[:width]), "row", 0)
    trailing = updated - exact_dot(lower_panel, upper_panel)
    return (
        lower_panel,
        upper_panel.reshape(width, 1, 1, width),
        trailing.reshape(local_rows, 1, 1, width),
    )


def solution(mesh):
    placed = (
        P("gz", "row", "col"),
        P("gz", "col", "row"),
        P("gz", None),
        P("row", "gz", "col", None),
    )
    return jax.shard_map(
        shards,
        mesh=mesh,
        in_specs=placed,
        out_specs=(P("row", None), P(None, "gz", "col", None), P("row", "gz", "col", None)),
        check_vma=False,
    )
```

profile of v0, /device:TPU:144, one launch (start us, length us, event | category | flops | bytes accessed | tf_op | source)
XLA Modules:
  0.0 487.4 jit_solution(1025770149250329940)
XLA Ops:
  8.0 0.0 all-gather.2.cloned.1.call-start
  8.0 0.7 convert_element_type.4
  8.7 0.1 dynamic-slice_bitcast_fusion
  8.8 0.1 broadcast_bitcast_fusion
  8.9 1.9 bitcast_multiply_fusion
  10.7 0.0 all-gather.2.cloned.1.call-update
  10.8 0.0 all-reduce.4.cloned.1.call-start
  10.8 1.8 fusion.1
  12.7 0.0 all-reduce.4.cloned.1.call-update
  12.7 0.0 reduce-scatter.2.cloned.1.call-start
  12.8 51.9 %all-gather.2.cloned.1.call-done = bf16[512,4096]{1,0:T(8,128)(2,1)} async-done(((bf16[512,512]{1,0:T(8,128)(2,1)}), bf16[512,4096]{1,0:T(8,128)(2,1)}) %all-gather.2.cloned.1.call-update) | async-done | bytes 4194320 | tf_op jit(solution)/shard_map/all_gather | solution.py:96
  64.7 0.0 copy-start
  64.7 6.5 %copy.7 = bf16[4096,512]{1,0:T(8,128)(2,1)} copy(bf16[4096,512]{0,1:T(8,128)(2,1)} %bitcast.36) | data formatting | bytes 8388608 | tf_op jit(solution)/shard_map/dot_general | solution.py:94
  71.2 0.0 copy-done
  71.2 6.9 %convolution_bitcast_fusion = f32[32,512,128]{2,1,0:T(8,128)} fusion(bf16[32,128,512]{2,1,0:T(8,128)(2,1)} %bitcast.35, bf16[1,512,512]{2,1,0:T(8,128)(2,1)S(1)} %copy-done, bf16[512]{0:T(512)(128)(2,1)S(1)} %broadcast_bitcast_fusion), kind=kOutput, calls=%fused_computation | convolution fusion | flops 2148532224 | bytes 13108224 | tf_op jit(solution)/shard_map/dot_general | solution.py:94
  78.1 0.0 copy-start.1
  78.1 0.0 reduce-scatter.2.cloned.1.call-update
  78.2 0.0 all-reduce.8.cloned.1.call-start
  78.2 192.9 %all-reduce.4.cloned.1.call-done.pivot = f32[128,128]{1,0:T(8,128)} async-done(((f32[128,128]{1,0:T(8,128)}), f32[128,128]{1,0:T(8,128)}) %all-reduce.4.cloned.1.call-update) | async-done | bytes 65552 | tf_op jit(solution)/shard_map/psum | solution.py:93
  271.1 15.9 %shard_map.67 = (f32[128,128]{1,0:T(8,128)}, f32[128,128]{1,0:T(8,128)}) custom-call(f32[128,128]{1,0:T(8,128)} %all-reduce.4.cloned.1.call-done.pivot), custom_call_target="tpu_custom_call" | custom-call | tf_op jit(solution)/shard_map/pallas_call | solution.py:63
  287.0 0.0 reduce-scatter.2.cloned.1.call-done
  287.0 0.0 copy-done.1
  287.0 1.0 bitcast_subtract_fusion
  288.0 1.7 convolution_select_fusion.1
  289.7 0.0 all-reduce.8.cloned.1.call-update
  289.7 0.0 all-reduce.6.cloned.1.call-start
  289.8 1.9 convolution_select_fusion
  291.7 0.0 all-reduce.6.cloned.1.call-update
  291.7 67.6 %all-reduce.8.cloned.1.call-done = f32[128,128]{1,0:T(8,128)} async-done(((f32[128,128]{1,0:T(8,128)}), f32[128,128]{1,0:T(8,128)}) %all-reduce.8.cloned.1.call-update) | async-done | bytes 65552 | tf_op jit(solution)/shard_map/psum | solution.py:72
  359.3 115.8 %all-reduce.6.cloned.1.call-done = f32[512,128]{1,0:T(8,128)} async-done(((f32[512,128]{1,0:T(8,128)}), f32[512,128]{1,0:T(8,128)}) %all-reduce.6.cloned.1.call-update) | async-done | bytes 262160 | tf_op jit(solution)/shard_map/psum | solution.py:72
  475.1 2.0 convolution_subtract_fusion
  477.1 1.7 copy.14
  478.8 1.5 copy.15
  (1 shorter events, 0.0 us)
Async XLA Ops:
  8.0 56.7 %all-gather.2.cloned.1.call-start = ((), (), s32[]{:S(2)}) async-start(), calls=%async_computation.1 | async-start | bytes 4718592 | tf_op jit(solution)/shard_map/all_gather | solution.py:96
  10.8 260.4 %all-reduce.4.cloned.1.call-start = ((), (), s32[]{:S(2)}) async-start(), calls=%async_computation.3 | async-start | bytes 131072 | tf_op jit(solution)/shard_map/psum | solution.py:93
  12.7 274.3 %reduce-scatter.2.cloned.1.call-start = ((), (), s32[]{:S(2)}) async-start(), calls=%async_computation.2 | async-start | bytes 8650752 | tf_op jit(solution)/shard_map/reduce_scatter | solution.py:100
  64.7 6.6 %copy-start = (bf16[1,512,512]{2,1,0:T(8,128)(2,1)S(1)}, bf16[1,512,512]{2,1,0:T(8,128)(2,1)}, u32[]{:S(2)}) copy-start(bf16[1,512,512]{2,1,0:T(8,128)(2,1)} %param.4) | copy-start | bytes 1572868
  78.1 208.9 %copy-start.1 = (f32[512,1,1,128]{3,2,1,0:T(1,128)S(1)}, f32[512,1,1,128]{3,2,1,0:T(1,128)}, u32[]{:S(2)}) copy-start(f32[512,1,1,128]{3,2,1,0:T(1,128)} %param.7) | copy-start | bytes 786436
  78.2 281.1 %all-reduce.8.cloned.1.call-start = ((), (), s32[]{:S(2)}) async-start(), calls=%async_computation.5 | async-start | bytes 131072 | tf_op jit(solution)/shard_map/psum | solution.py:72
  289.7 185.4 %all-reduce.6.cloned.1.call-start = ((), (), s32[]{:S(2)}) async-start(), calls=%async_computation.4 | async-start | bytes 524288 | tf_op jit(solution)/shard_map/psum | solution.py:72
Sparse Core Ops, SparseCore 0:
  10.9 53.7 all-gather.1
  78.3 101.4 reduce-scatter.1
  289.8 69.3 all-reduce.7
  362.9 112.1 all-reduce.5
Sparse Core Ops, SparseCore 1:
  18.2 252.8 all-reduce.3
where the time goes:
time: 491 us; the launch traced here: 487 us
  waiting for transfers between devices  428 us (87%)
  Pallas kernels  15.9 us (3%)
  between operations  15.3 us (3%)
  matrix products  14.4 us (3%)
  local copies, waits for them, and re-layouts  9.85 us (2%)
    psum x1, waiting for transfers between devices, shards(): lax.psum(pivot_term, ('gz', 'row', 'col'))  193 us
    psum x2, waiting for transfers between devices, broadcast(): return lax.psum(jnp.where(mine, shard, jnp.zeros_like(shard)), axis)  183 us
    all_gather x1, waiting for transfers between devices, shards(): lax.all_gather(upper_kept, 'row', axis=1, tiled=True)  51.9 us
    pallas_call x1, Pallas kernels, factor(): pl.pallas_call(factor_kernel, out_shape=(square, square), scratch_shapes=...  15.9 us
  transfers between devices with their start and end apart: 5, of which 4 were waited for; matrix products, arithmetic and copies ran while one was open for 4% of the time, Pallas kernels for 3%

commit v1 on v0

v1 whole, which is shorter than its diff:
```python
import functools

import jax
import jax.numpy as jnp
from jax import lax
from jax.experimental import pallas as pl
from jax.experimental.pallas import tpu as pltpu
from jax.sharding import PartitionSpec as P

BLOCK = 128
MESH = pl.DeviceIdType.MESH
ORDER_OF_K = (0, 1, 3, 2)


def exact_dot(left, right):
    return jnp.dot(
        left, right, precision=lax.Precision.HIGHEST, preferred_element_type=jnp.float32
    )


def eliminate(first, count, worked, product, lower, lower_inverse):
    rows = lax.broadcasted_iota(jnp.int32, (BLOCK, BLOCK), 0)
    lanes = lax.broadcasted_iota(jnp.int32, (BLOCK, BLOCK), 1)

    def step(at, carry):
        dense = worked[...]
        pivot_row = worked[pl.ds(at, 1), :]
        product_row = product[pl.ds(at, 1), :]
        lower_inverse[pl.ds(at, 1), :] = product_row
        column = jnp.sum(jnp.where(lanes == at, dense, 0.0), axis=1, keepdims=True)
        pivot = jnp.sum(
            jnp.where(lanes[:1] == at, pivot_row, 0.0), axis=1, keepdims=True
        )
        scaled = jnp.where(rows == at, 0.0, column / pivot)
        worked[...] = dense - scaled * pivot_row
        product[...] = product[...] - scaled * product_row
        lower[...] = jnp.where((lanes == at) & (rows > at), scaled, lower[...])
        return carry

    lax.fori_loop(first, first + count, step, 0)


def start_elimination(pivot, worked, product, lower):
    rows = lax.broadcasted_iota(jnp.int32, (BLOCK, BLOCK), 0)
    lanes = lax.broadcasted_iota(jnp.int32, (BLOCK, BLOCK), 1)
    identity = jnp.where(rows == lanes, 1.0, 0.0)
    worked[...] = pivot
    product[...] = identity
    lower[...] = identity


def finish_elimination(worked, product, lower):
    rows = lax.broadcasted_iota(jnp.int32, (BLOCK, BLOCK), 0)
    lanes = lax.broadcasted_iota(jnp.int32, (BLOCK, BLOCK), 1)
    pivots = jnp.sum(jnp.where(rows == lanes, worked[...], 0.0), axis=1, keepdims=True)
    return exact_dot(product[...] / pivots, lower[...])


def remote(src, dst, send_sem, recv_sem, **where):
    return pltpu.make_async_remote_copy(
        src_ref=src,
        dst_ref=dst,
        send_sem=send_sem,
        recv_sem=recv_sem,
        device_id=where,
        device_id_type=MESH,
    )


def front_kernel(
    n_gz, n_row, n_col,
    lower_in, upper_in, touched, front,
    lower_panel, upper_panel, trailing,
    lowers, uppers, gathered, terms, arrived,
    first_rows, first_columns, pivot_front, row_front,
    split, split_in, summed, summed_in, row_in, panel, row_panel,
    worked, product, lower_unit, lower_inverse,
    up_send, up_recv, low_send, low_recv, z_send, z_recv, term_send, term_recv,
    chain_send, chain_recv, row_front_sem, split_send, split_recv, summed_send, summed_recv,
    row_send, row_recv, panel_send, panel_recv, spread_send, spread_recv,
):
    g, r, c = lax.axis_index("gz"), lax.axis_index("row"), lax.axis_index("col")
    height = lower_in.shape[0]
    panels = height // BLOCK
    half = height // 2

    def gz(step):
        return lax.rem(g + step, n_gz)

    def row(step):
        return lax.rem(r + n_row + step, n_row)

    def col(step):
        return lax.rem(c + n_col + step, n_col)

    barrier = pltpu.get_barrier_semaphore()
    for step in range(1, n_gz):
        pl.semaphore_signal(barrier, inc=1, device_id={"gz": gz(step)}, device_id_type=MESH)
    for step in range(1, n_row):
        pl.semaphore_signal(barrier, inc=1, device_id={"row": row(step)}, device_id_type=MESH)
    for step in range(1, n_col):
        pl.semaphore_signal(barrier, inc=1, device_id={"col": col(step)}, device_id_type=MESH)

    for at in range(panels):
        mark = touched[0, r * panels + at].astype(jnp.float32)
        span = pl.ds(at * BLOCK, BLOCK)
        uppers[at] = (upper_in[:, span].astype(jnp.float32) * mark).astype(jnp.bfloat16)
        lowers[c, span, :] = (lower_in[span, :].astype(jnp.float32) * mark).astype(jnp.bfloat16)
    gathered[r, c] = uppers[c]

    @pl.when(r == 0)
    def _():
        first_rows[...] = lowers[c, :BLOCK, :]
        first_columns[...] = uppers[0]
        pivot_front[...] = front[:BLOCK, :]

    @pl.when((r == 0) & (g == 0))
    def _():
        row_front[...] = front[:BLOCK, :]

    pl.semaphore_wait(barrier, n_gz + n_row + n_col - 3)

    corner = (g == 0) & (c == 0)

    def chain(way, at):
        slot = 0 if way > 0 else 1
        buffers = (first_columns, first_rows, pivot_front)
        return remote(
            buffers[at], buffers[at], chain_send.at[slot, at], chain_recv.at[at], row=row(way)
        )

    def chain_start(way):
        chain(way, 0).start()
        chain(way, 1).start()

        @pl.when(corner)
        def _():
            chain(way, 2).start()

    def chain_arrive():
        chain(1, 0).wait_recv()
        chain(1, 1).wait_recv()

        @pl.when(corner)
        def _():
            chain(1, 2).wait_recv()

    def chain_sent(way):
        chain(way, 0).wait_send()
        chain(way, 1).wait_send()

        @pl.when(corner)
        def _():
            chain(way, 2).wait_send()

    def row_front_copy():
        return remote(
            front.at[pl.ds(0, BLOCK), :], row_front, row_front_sem.at[0], row_front_sem.at[1], row=g
        )

    def chain_hop(hop):
        @pl.when(r == hop)
        def _():
            chain_arrive()
            if hop < n_row // 2:
                chain_start(1)

        if hop < n_row // 2:
            @pl.when(r == n_row - hop)
            def _():
                chain_arrive()
                if hop < n_row // 2 - 1:
                    chain_start(-1)

    @pl.when(r == 0)
    def _():
        chain_start(1)
        chain_start(-1)

    up_copies = []
    for slot, step in enumerate(ORDER_OF_K[1:]):
        up_copies.append(
            remote(
                uppers.at[col(step)], gathered.at[r, c], up_send.at[slot], up_recv.at[c], col=col(step)
            )
        )

    def up_arrive(step):
        remote(
            uppers.at[0], gathered.at[r, col(step)], up_send.at[0], up_recv.at[col(step)], col=col(step)
        ).wait_recv()

    def z_copy(way, distance, place):
        source = row(-way * distance)
        k_block = col(ORDER_OF_K[place])
        piece = gathered.at[source, k_block]
        slot = 0 if way > 0 else 1
        at = distance * n_col + place
        return remote(piece, piece, z_send.at[slot, at], z_recv.at[source, k_block], row=row(way))

    last = n_row // 2 - 1
    z_order = [(distance, place) for distance in range(last) for place in range(n_col)]
    z_order += [(last, place) for place in range(n_col // 2)]
    z_copies = []

    def z_step(at):
        distance, place = z_order[at]
        if distance == 0 and place > 0:
            up_arrive(ORDER_OF_K[place])
        for way in (1, -1):
            used = place
            if distance == last and way < 0:
                used = place + n_col // 2
            copy = z_copy(way, distance, used)
            if distance > 0:
                copy.wait_recv()
            copy.start()
            z_copies.append(copy)

    def low_copy(way):
        slot = 0 if way > 0 else 1
        return remote(
            lowers.at[c], lowers.at[c], low_send.at[slot], low_recv.at[slot], col=col(way)
        )

    def low_pass(way):
        slot = 0 if way > 0 else 1
        piece = lowers.at[col(-way), pl.ds(slot * half, half), :]
        return remote(piece, piece, low_send.at[2 + slot], low_recv.at[2 + slot], col=col(way))

    def low_wait(way):
        slot = 0 if way > 0 else 1
        block = lowers.at[col(-way)]
        remote(block, block, low_send.at[slot], low_recv.at[slot], col=col(way)).wait_recv()

    def low_far_wait(way):
        slot = 0 if way > 0 else 1
        piece = lowers.at[col(2), pl.ds(slot * half, half), :]
        remote(piece, piece, low_send.at[2 + slot], low_recv.at[2 + slot], col=col(way)).wait_recv()

    for copy in up_copies:
        copy.start()
    z_step(0)
    for way in (1, -1):
        low_copy(way).start()

    @pl.when((r == 0) & (g != 0))
    def _():
        row_front_copy().start()

    for hop in range(1, n_row // 2 + 1):
        chain_hop(hop)
        if hop < n_col:
            z_step(hop)

    column = first_columns[...]
    pivot_part = jnp.dot(first_rows[...], column, preferred_element_type=jnp.float32)
    sums, backs = BLOCK // n_col + BLOCK, BLOCK // n_col
    for at in range(n_col):
        split[at, :backs] = -pivot_part[at * backs : (at + 1) * backs]
        split[at, backs:sums] = -jnp.dot(
            lowers[c, at * BLOCK : (at + 1) * BLOCK, :], column, preferred_element_type=jnp.float32
        )
        split[at, sums:] = -jnp.dot(
            first_rows[...], uppers[at], preferred_element_type=jnp.float32
        )

    @pl.when(corner)
    def _():
        for at in range(n_col):
            split[at, :backs] += pivot_front[at * backs : (at + 1) * backs, :]
            split[at, backs:sums] += front[at * BLOCK : (at + 1) * BLOCK, :]

    split_copies = []
    for step in range(1, n_col):
        copy = remote(
            split.at[col(step)], split_in.at[c], split_send.at[step], split_recv.at[c], col=col(step)
        )
        copy.start()
        split_copies.append(copy)
    z_step(4)
    z_step(5)

    for step in range(1, n_col):
        remote(
            split.at[0], split_in.at[col(step)], split_send.at[0], split_recv.at[col(step)], col=col(step)
        ).wait_recv()
    summed[...] = (split[c] + split_in[col(1)]) + (split_in[col(2)] + split_in[col(3)])
    summed_copies = []
    for step in range(1, n_gz):
        copy = remote(
            summed.at[pl.ds(0, sums), :], summed_in.at[g], summed_send.at[step], summed_recv.at[g], gz=gz(step)
        )
        copy.start()
        summed_copies.append(copy)

    def row_copy():
        return remote(summed.at[pl.ds(sums, BLOCK), :], row_in.at[g], row_send, row_recv.at[g], gz=r)

    @pl.when(g != r)
    def _():
        row_copy().start()

    z_step(6)
    z_step(7)
    for way in (1, -1):
        low_wait(way)
        low_pass(way).start()

    for step in range(1, n_gz):
        remote(
            summed.at[pl.ds(0, sums), :], summed_in.at[gz(step)], summed_send.at[0], summed_recv.at[gz(step)], gz=gz(step)
        ).wait_recv()
    total = summed[:sums, :]
    for step in range(1, n_gz):
        total += summed_in[gz(step)]
    panel[c] = total
    panel_copies = []
    for step in range(1, n_col):
        copy = remote(panel.at[c], panel.at[c], panel_send.at[step], panel_recv.at[c], col=col(step))
        copy.start()
        panel_copies.append(copy)

    def spread_copy(step):
        return remote(row_panel, row_panel, spread_send.at[step], spread_recv, row=row(step))

    @pl.when(g == r)
    def _():
        @pl.when(g != 0)
        def _():
            row_front_copy().wait_recv()

        total = summed[sums:, :] + row_front[...]
        for step in range(1, n_gz):
            remote(
                summed.at[pl.ds(sums, BLOCK), :], row_in.at[gz(step)], row_send, row_recv.at[gz(step)], gz=gz(step)
            ).wait_recv()
            total += row_in[gz(step)]
        row_panel[...] = total
        for step in range(1, n_row):
            spread_copy(step).start()

    z_step(8)
    z_step(9)
    for step in range(1, n_col):
        piece = panel.at[col(step)]
        remote(piece, piece, panel_send.at[0], panel_recv.at[col(step)], col=col(step)).wait_recv()
    pivot = jnp.concatenate([panel[at, :backs] for at in range(n_col)], axis=0)
    start_elimination(pivot, worked, product, lower_unit)
    pace = BLOCK // 8

    def factor_part(at):
        eliminate(at * pace, pace, worked, product, lower_unit, lower_inverse)

    def term_copy(j):
        return remote(terms.at[j], arrived.at[g], term_send.at[j], term_recv.at[g], gz=j)

    def term(distance):
        j = row(distance)
        for at in range(2):
            span = pl.ds(at * half, half)
            total = jnp.dot(lowers[0, span, :], gathered[j, 0], preferred_element_type=jnp.float32)
            for k_block in range(1, n_col):
                total += jnp.dot(
                    lowers[k_block, span, :], gathered[j, k_block], preferred_element_type=jnp.float32
                )
            terms[j, span, :] = total

        @pl.when(j != g)
        def _():
            term_copy(j).start()

    factor_part(0)
    z_step(10)
    z_step(11)
    factor_part(1)
    for way in (1, -1):
        low_far_wait(way)
    term(0)
    term(1)
    term(-1)
    factor_part(2)
    z_step(12)
    z_step(13)
    factor_part(3)
    term(2)
    term(-2)
    for at in range(4, 8):
        factor_part(at)

    for way in (1, -1):
        for place in range(n_col // 2):
            z_copy(way, last, place + (n_col // 2 if way > 0 else 0)).wait_recv()
    term(3)
    term(-3)

    upper_inverse = finish_elimination(worked, product, lower_unit)

    @pl.when(g != r)
    def _():
        spread_copy(1).wait_recv()

    upper = exact_dot(lower_inverse[...], row_panel[...])
    upper_panel[...] = upper
    for at in range(panels):
        span = pl.ds(at * BLOCK, BLOCK)
        lower = exact_dot(panel[at, backs:, :], upper_inverse)
        lower_panel[span, :] = lower
        trailing[span, :] = front[span, :] - exact_dot(lower, upper)

    for way in (1, -1):
        for place in range(n_col // 2):
            z_copy(way, last + 1, place + (0 if way > 0 else n_col // 2)).wait_recv()
    term(last + 1)

    for step in range(1, n_gz):
        block = arrived.at[gz(step)]
        remote(block, block, term_send.at[0], term_recv.at[gz(step)], gz=gz(step)).wait_recv()

    def add_up(at, carry):
        span = pl.ds(pl.multiple_of(at * BLOCK, BLOCK), BLOCK)
        total = terms[g, span, :]
        for step in range(1, n_gz):
            total += arrived[gz(step), span, :]
        trailing[span, :] -= total
        return carry

    lax.fori_loop(0, panels, add_up, 0)

    for copy in up_copies + z_copies + split_copies + summed_copies + panel_copies:
        copy.wait_send()
    for way in (1, -1):
        low_copy(way).wait_send()
        low_pass(way).wait_send()
    for step in range(1, n_gz):
        term_copy(gz(step)).wait_send()

    @pl.when(r < n_row // 2)
    def _():
        chain_sent(1)

    @pl.when((r == 0) | (r > n_row // 2 + 1))
    def _():
        chain_sent(-1)

    @pl.when((r == 0) & (g != 0))
    def _():
        row_front_copy().wait_send()

    @pl.when(g != r)
    def _():
        row_copy().wait_send()

    @pl.when(g == r)
    def _():
        for step in range(1, n_row):
            spread_copy(step).wait_send()


def shards(n_gz, n_row, n_col, subtree_lower, subtree_upper, touched, front):
    height, depth = subtree_lower.shape[1:]
    width = front.shape[3]
    bf16, f32 = jnp.bfloat16, jnp.float32
    dma = pltpu.SemaphoreType.DMA
    backs = BLOCK // n_col
    vmem = pl.BlockSpec(memory_space=pltpu.VMEM)
    lower_panel, upper_panel, trailing = pl.pallas_call(
        functools.partial(front_kernel, n_gz, n_row, n_col),
        out_shape=(
            jax.ShapeDtypeStruct((height, width), f32),
            jax.ShapeDtypeStruct((width, width), f32),
            jax.ShapeDtypeStruct((height, width), f32),
        ),
        in_specs=[vmem, vmem, pl.BlockSpec(memory_space=pltpu.SMEM), vmem],
        out_specs=(vmem, vmem, vmem),
        scratch_shapes=[
            pltpu.VMEM((n_col, height, depth), bf16),
            pltpu.VMEM((n_col, depth, BLOCK), bf16),
            pltpu.VMEM((n_row, n_col, depth, BLOCK), bf16),
            pltpu.VMEM((n_gz, height, BLOCK), f32),
            pltpu.VMEM((n_gz, height, BLOCK), f32),
            pltpu.VMEM((BLOCK, depth), bf16),
            pltpu.VMEM((depth, BLOCK), bf16),
            pltpu.VMEM((BLOCK, BLOCK), f32),
            pltpu.VMEM((BLOCK, BLOCK), f32),
            pltpu.VMEM((n_col, backs + 2 * BLOCK, BLOCK), f32),
            pltpu.VMEM((n_col, backs + 2 * BLOCK, BLOCK), f32),
            pltpu.VMEM((backs + 2 * BLOCK, BLOCK), f32),
            pltpu.VMEM((n_gz, backs + BLOCK, BLOCK), f32),
            pltpu.VMEM((n_gz, BLOCK, BLOCK), f32),
            pltpu.VMEM((n_col, backs + BLOCK, BLOCK), f32),
            pltpu.VMEM((BLOCK, BLOCK), f32),
            pltpu.VMEM((BLOCK, BLOCK), f32),
            pltpu.VMEM((BLOCK, BLOCK), f32),
            pltpu.VMEM((BLOCK, BLOCK), f32),
            pltpu.VMEM((BLOCK, BLOCK), f32),
            dma((n_col,)), dma((n_col,)),
            dma((4,)), dma((4,)),
            dma((2, n_row * n_col)), dma((n_row, n_col)),
            dma((n_gz,)), dma((n_gz,)),
            dma((2, 3)), dma((3,)),
            dma((2,)),
            dma((n_col,)), dma((n_col,)),
            dma((n_gz,)), dma((n_gz,)),
            dma, dma((n_gz,)),
            dma((n_col,)), dma((n_col,)),
            dma((n_row,)), dma,
        ],
        compiler_params=pltpu.CompilerParams(
            collective_id=0, has_side_effects=True, vmem_limit_bytes=48 * 1024 * 1024
        ),
    )(subtree_lower[0], subtree_upper[0], touched, front.reshape(height, width))
    return (
        lower_panel,
        upper_panel.reshape(width, 1, 1, width),
        trailing.reshape(height, 1, 1, width),
    )


def solution(mesh):
    placed = (
        P("gz", "row", "col"),
        P("gz", "col", "row"),
        P("gz", None),
        P("row", "gz", "col", None),
    )
    return jax.shard_map(
        functools.partial(shards, mesh.shape["gz"], mesh.shape["row"], mesh.shape["col"]),
        mesh=mesh,
        in_specs=placed,
        out_specs=(P("row", None), P(None, "gz", "col", None), P("row", "gz", "col", None)),
        check_vma=False,
    )
```

time: 491 us -> 110 us (0.22)
  the two profiles are of different devices: /device:TPU:144 before, /device:TPU:103 now
where the time goes in v1:
time: 110 us
  Pallas kernels  104 us (95%)
  local copies, waits for them, and re-layouts  5.72 us (5%)
    pallas_call x1, Pallas kernels, shards(): pl.pallas_call(functools.partial(front_kernel, n_gz, n_row, n_col), out_s...  104 us
    unnamed x11, local copies, waits for them, and re-layouts  5.72 us

profile of v1, /device:TPU:103, one launch (start us, length us, event | category | flops | bytes accessed | tf_op | source)
XLA Modules:
  0.0 110.0 jit_solution(18435484905060016042)
XLA Ops:
  0.6 0.0 copy-start.3
  0.6 0.6 copy-done.3
  1.3 0.0 copy-start
  1.3 1.0 copy-done
  2.3 0.0 copy-start.1
  2.3 1.0 copy-done.1
  3.4 0.0 copy-start.2
  3.4 0.9 copy-done.2
  4.3 103.6 %shard_map.67 = (f32[512,128]{1,0:T(8,128)S(1)}, f32[128,128]{1,0:T(8,128)S(1)}, f32[512,128]{1,0:T(8,128)S(1)}) custom-call(bf16[512,512]{1,0:T(8,128)(2,1)S(1)} %bitcast.9, bf16[512,512]{1,0:T(8,128)(2,1)S(1)} %bitcast.10, s32[1,32]{1,0:T(1,128)S(1)} %copy-done.3, f32[512,128]{1,0:T(8,128)S(1)} %bitcast.11), custom_call_target="tpu_custom_call" | custom-call | tf_op jit(solution)/shard_map/pallas_call | solution.py:467
  107.9 0.7 copy.12
  108.6 0.6 copy.13
  109.3 0.7 copy.14
Async XLA Ops:
  0.6 0.7 copy-start.3
  1.3 1.0 copy-start
  2.3 1.0 copy-start.1
  3.4 0.9 copy-start.2

commit v2 on v1

v2 whole, which is shorter than its diff:
```python
import functools

import jax
import jax.numpy as jnp
from jax import lax
from jax.experimental import pallas as pl
from jax.experimental.pallas import tpu as pltpu
from jax.sharding import PartitionSpec as P

BLOCK = 128
MESH = pl.DeviceIdType.MESH
ORDER_OF_K = (0, 1, 3, 2)


def exact_dot(left, right):
    return jnp.dot(
        left, right, precision=lax.Precision.HIGHEST, preferred_element_type=jnp.float32
    )


def eliminate(first, count, worked, product, lower, lower_inverse):
    rows = lax.broadcasted_iota(jnp.int32, (BLOCK, BLOCK), 0)
    lanes = lax.broadcasted_iota(jnp.int32, (BLOCK, BLOCK), 1)

    def step(at, carry):
        dense = worked[...]
        pivot_row = worked[pl.ds(at, 1), :]
        product_row = product[pl.ds(at, 1), :]
        lower_inverse[pl.ds(at, 1), :] = product_row
        column = jnp.sum(jnp.where(lanes == at, dense, 0.0), axis=1, keepdims=True)
        pivot = jnp.sum(
            jnp.where(lanes[:1] == at, pivot_row, 0.0), axis=1, keepdims=True
        )
        scaled = jnp.where(rows == at, 0.0, column / pivot)
        worked[...] = dense - scaled * pivot_row
        product[...] = product[...] - scaled * product_row
        lower[...] = jnp.where((lanes == at) & (rows > at), scaled, lower[...])
        return carry

    lax.fori_loop(first, first + count, step, 0)


def start_elimination(pivot, worked, product, lower):
    rows = lax.broadcasted_iota(jnp.int32, (BLOCK, BLOCK), 0)
    lanes = lax.broadcasted_iota(jnp.int32, (BLOCK, BLOCK), 1)
    identity = jnp.where(rows == lanes, 1.0, 0.0)
    worked[...] = pivot
    product[...] = identity
    lower[...] = identity


def finish_elimination(worked, product, lower):
    rows = lax.broadcasted_iota(jnp.int32, (BLOCK, BLOCK), 0)
    lanes = lax.broadcasted_iota(jnp.int32, (BLOCK, BLOCK), 1)
    pivots = jnp.sum(jnp.where(rows == lanes, worked[...], 0.0), axis=1, keepdims=True)
    return exact_dot(product[...] / pivots, lower[...])


def remote(src, dst, send_sem, recv_sem, **where):
    return pltpu.make_async_remote_copy(
        src_ref=src,
        dst_ref=dst,
        send_sem=send_sem,
        recv_sem=recv_sem,
        device_id=where,
        device_id_type=MESH,
    )


def front_kernel(
    n_gz, n_row, n_col,
    lower_hbm, upper_hbm, touched_hbm, front_hbm,
    lower_panel, upper_panel, trailing,
    lower_in, upper_in, touched, front,
    lowers, uppers, gathered, terms, pair_out, pair_in, arrived,
    first_rows, first_columns, row_front,
    pivot_split, pivot_split_in, pivot_sum, pivot_sum_in, pivot,
    split, split_in, summed, summed_in, row_in, panel, row_panel,
    worked, product, lower_unit, lower_inverse,
    in_sem, up_send, up_recv, low_send, low_recv, z_send, z_recv, term_send, term_recv,
    pair_send, pair_recv, chain_send, chain_recv, row_front_sem,
    pivot_split_send, pivot_split_recv, pivot_sum_send, pivot_sum_recv,
    pivot_row_send, pivot_row_recv, pivot_col_send, pivot_col_recv,
    split_send, split_recv, summed_send, summed_recv,
    row_send, row_recv, panel_send, panel_recv, spread_send, spread_recv,
):
    g, r, c = lax.axis_index("gz"), lax.axis_index("row"), lax.axis_index("col")
    height = lower_in.shape[0]
    panels = height // BLOCK
    half = height // 2
    backs = BLOCK // n_col
    x, core = g // 2, lax.rem(g, 2)
    sibling = g + 1 - 2 * core
    sends = []

    def gz(step):
        return lax.rem(g + step, n_gz)

    def row(step):
        return lax.rem(r + n_row + step, n_row)

    def col(step):
        return lax.rem(c + n_col + step, n_col)

    def start(copy):
        copy.start()
        sends.append(copy)

    inputs = [
        pltpu.make_async_copy(upper_hbm, upper_in, in_sem.at[0]),
        pltpu.make_async_copy(touched_hbm, touched, in_sem.at[1]),
        pltpu.make_async_copy(lower_hbm, lower_in, in_sem.at[2]),
        pltpu.make_async_copy(front_hbm, front, in_sem.at[3]),
    ]
    for copy in inputs:
        copy.start()

    barrier = pltpu.get_barrier_semaphore()
    for step in range(1, n_gz):
        pl.semaphore_signal(barrier, inc=1, device_id={"gz": gz(step)}, device_id_type=MESH)
    for step in range(1, n_row):
        pl.semaphore_signal(barrier, inc=1, device_id={"row": row(step)}, device_id_type=MESH)
    for step in range(1, n_col):
        pl.semaphore_signal(barrier, inc=1, device_id={"col": col(step)}, device_id_type=MESH)

    for copy in inputs:
        copy.wait()
    for at in range(panels):
        mark = touched[0, r * panels + at].astype(jnp.float32)
        span = pl.ds(at * BLOCK, BLOCK)
        uppers[at] = (upper_in[:, span].astype(jnp.float32) * mark).astype(jnp.bfloat16)
        lowers[c, span, :] = (lower_in[span, :].astype(jnp.float32) * mark).astype(jnp.bfloat16)
    gathered[r, c] = uppers[c]
    corner = (g == 0) & (c == 0)

    @pl.when(r == 0)
    def _():
        first_rows[...] = lowers[c, :BLOCK, :]
        first_columns[...] = uppers[0]
        part = -jnp.dot(lowers[c, :BLOCK, :], uppers[0], preferred_element_type=jnp.float32)
        for at in range(n_col):
            pivot_split[at] = part[at * backs : (at + 1) * backs]

    @pl.when((r == 0) & (g == 0))
    def _():
        row_front[...] = front[:BLOCK, :]

    @pl.when((r == 0) & corner)
    def _():
        for at in range(n_col):
            pivot_split[at] += front[at * backs : (at + 1) * backs, :]

    pl.semaphore_wait(barrier, n_gz + n_row + n_col - 3)

    def pivot_split_copy(step):
        return remote(
            pivot_split.at[col(step)], pivot_split_in.at[c],
            pivot_split_send.at[step], pivot_split_recv.at[c], col=col(step),
        )

    def pivot_sum_copy(step):
        return remote(
            pivot_sum, pivot_sum_in.at[g], pivot_sum_send.at[step], pivot_sum_recv.at[g], gz=gz(step)
        )

    def pivot_row_copy(step):
        piece = pivot.at[c]
        return remote(piece, piece, pivot_row_send.at[step], pivot_row_recv, row=row(step))

    def pivot_over_col():
        @pl.when(r == 0)
        def _():
            for step in range(1, n_col):
                remote(
                    pivot_split.at[0], pivot_split_in.at[col(step)],
                    pivot_split_send.at[0], pivot_split_recv.at[col(step)], col=col(step),
                ).wait_recv()
            total = pivot_split[c]
            for step in range(1, n_col):
                total += pivot_split_in[col(step)]
            pivot_sum[...] = total
            for step in range(1, n_gz):
                pivot_sum_copy(step).start()

    def pivot_over_gz():
        @pl.when(r == 0)
        def _():
            for step in range(1, n_gz):
                remote(
                    pivot_sum, pivot_sum_in.at[gz(step)],
                    pivot_sum_send.at[0], pivot_sum_recv.at[gz(step)], gz=gz(step),
                ).wait_recv()
            total = pivot_sum[...]
            for step in range(1, n_gz):
                total += pivot_sum_in[gz(step)]
            pivot[c] = total
            for step in range(1, n_row):
                pivot_row_copy(step).start()

    def pivot_out():
        @pl.when(r != 0)
        def _():
            pivot_row_copy(1).wait_recv()

        for step in range(1, n_col):
            piece = pivot.at[c]
            start(remote(piece, piece, pivot_col_send.at[step], pivot_col_recv.at[c], col=col(step)))

    def pivot_done():
        for step in range(1, n_col):
            piece = pivot.at[col(step)]
            remote(
                piece, piece, pivot_col_send.at[0], pivot_col_recv.at[col(step)], col=col(step)
            ).wait_recv()
        whole = jnp.concatenate([pivot[at] for at in range(n_col)], axis=0)
        start_elimination(whole, worked, product, lower_unit)

    def chain(way, at):
        slot = 0 if way > 0 else 1
        buffer = (first_columns, first_rows)[at]
        return remote(buffer, buffer, chain_send.at[slot, at], chain_recv.at[at], row=row(way))

    def chain_hop(hop):
        def pass_on(way):
            for at in range(2):
                chain(1, at).wait_recv()
                if way:
                    chain(way, at).start()

        @pl.when(r == hop)
        def _():
            pass_on(1 if hop < n_row // 2 else 0)

        if hop < n_row // 2:
            @pl.when(r == n_row - hop)
            def _():
                pass_on(-1 if hop < n_row // 2 - 1 else 0)

    def row_front_copy():
        return remote(
            front.at[pl.ds(0, BLOCK), :], row_front, row_front_sem.at[0], row_front_sem.at[1], row=g
        )

    def up_arrive(step):
        remote(
            uppers.at[0], gathered.at[r, col(step)], up_send.at[0], up_recv.at[col(step)], col=col(step)
        ).wait_recv()

    def z_copy(way, distance, place):
        source = row(-way * distance)
        k_block = col(ORDER_OF_K[place])
        piece = gathered.at[source, k_block]
        slot = 0 if way > 0 else 1
        at = distance * n_col + place
        return remote(piece, piece, z_send.at[slot, at], z_recv.at[source, k_block], row=row(way))

    last = n_row // 2 - 1
    z_order = [(distance, place) for distance in range(last) for place in range(n_col)]
    z_order += [(last, place) for place in range(n_col // 2)]

    def z_step(at):
        distance, place = z_order[at]
        if distance == 0 and place > 0:
            up_arrive(ORDER_OF_K[place])
        for way in (1, -1):
            used = place
            if distance == last and way < 0:
                used = place + n_col // 2
            copy = z_copy(way, distance, used)
            if distance > 0:
                copy.wait_recv()
            start(copy)

    def low_copy(way):
        slot = 0 if way > 0 else 1
        return remote(
            lowers.at[c], lowers.at[c], low_send.at[slot], low_recv.at[slot], col=col(way)
        )

    def low_pass(way):
        slot = 0 if way > 0 else 1
        block = lowers.at[col(-way)]
        remote(block, block, low_send.at[slot], low_recv.at[slot], col=col(way)).wait_recv()
        piece = lowers.at[col(-way), pl.ds(slot * half, half), :]
        start(remote(piece, piece, low_send.at[2 + slot], low_recv.at[2 + slot], col=col(way)))

    def low_far_wait(way):
        slot = 0 if way > 0 else 1
        piece = lowers.at[col(2), pl.ds(slot * half, half), :]
        remote(piece, piece, low_send.at[2 + slot], low_recv.at[2 + slot], col=col(way)).wait_recv()

    def panel_products():
        column = first_columns[...]
        for at in range(n_col):
            split[at, :BLOCK] = -jnp.dot(
                lowers[c, at * BLOCK : (at + 1) * BLOCK, :], column, preferred_element_type=jnp.float32
            )
            split[at, BLOCK:] = -jnp.dot(
                first_rows[...], uppers[at], preferred_element_type=jnp.float32
            )

        @pl.when(corner)
        def _():
            for at in range(n_col):
                split[at, :BLOCK] += front[at * BLOCK : (at + 1) * BLOCK, :]

        for step in range(1, n_col):
            start(
                remote(
                    split.at[col(step)], split_in.at[c],
                    split_send.at[step], split_recv.at[c], col=col(step),
                )
            )

    def row_copy():
        return remote(summed.at[pl.ds(BLOCK, BLOCK), :], row_in.at[g], row_send, row_recv.at[g], gz=r)

    def panel_over_col():
        for step in range(1, n_col):
            remote(
                split.at[0], split_in.at[col(step)],
                split_send.at[0], split_recv.at[col(step)], col=col(step),
            ).wait_recv()
        total = split[c]
        for step in range(1, n_col):
            total += split_in[col(step)]
        summed[...] = total

        @pl.when(g != r)
        def _():
            row_copy().start()

        for step in range(1, n_gz):
            start(
                remote(
                    summed.at[pl.ds(0, BLOCK), :], summed_in.at[g],
                    summed_send.at[step], summed_recv.at[g], gz=gz(step),
                )
            )

    def spread_copy(step):
        return remote(row_panel, row_panel, spread_send.at[step], spread_recv, row=row(step))

    def panel_over_gz():
        @pl.when(g == r)
        def _():
            @pl.when(g != 0)
            def _():
                row_front_copy().wait_recv()

            total = summed[BLOCK:, :] + row_front[...]
            for step in range(1, n_gz):
                remote(
                    summed.at[pl.ds(BLOCK, BLOCK), :], row_in.at[gz(step)],
                    row_send, row_recv.at[gz(step)], gz=gz(step),
                ).wait_recv()
                total += row_in[gz(step)]
            row_panel[...] = total
            for step in range(1, n_row):
                spread_copy(step).start()

        total = summed[:BLOCK, :]
        for step in range(1, n_gz):
            remote(
                summed.at[pl.ds(0, BLOCK), :], summed_in.at[gz(step)],
                summed_send.at[0], summed_recv.at[gz(step)], gz=gz(step),
            ).wait_recv()
            total += summed_in[gz(step)]
        panel[c] = total
        for step in range(1, n_col):
            start(
                remote(panel.at[c], panel.at[c], panel_send.at[step], panel_recv.at[c], col=col(step))
            )

    def panel_done():
        for step in range(1, n_col):
            piece = panel.at[col(step)]
            remote(piece, piece, panel_send.at[0], panel_recv.at[col(step)], col=col(step)).wait_recv()

        @pl.when(g != r)
        def _():
            spread_copy(1).wait_recv()

    done = [0]

    def factor_part(count):
        eliminate(done[0], count, worked, product, lower_unit, lower_inverse)
        done[0] += count

    def term_copy(j):
        span = pl.ds(pl.multiple_of(core * half, half), half)
        return remote(terms.at[j], arrived.at[x, span, :], term_send.at[j], term_recv.at[g], gz=j)

    def layer_rows(j, which):
        span = pl.ds(pl.multiple_of(which * half, half), half)
        total = jnp.dot(lowers[0, span, :], gathered[j, 0], preferred_element_type=jnp.float32)
        for k_block in range(1, n_col):
            total += jnp.dot(
                lowers[k_block, span, :], gathered[j, k_block], preferred_element_type=jnp.float32
            )
        return total

    def pair_copy(j):
        return remote(pair_out.at[j], pair_in.at[j], pair_send.at[j], pair_recv.at[j], gz=sibling)

    def term(distance):
        j = row(distance)
        pair_out[j] = layer_rows(j, 1 - core)
        start(pair_copy(j))
        terms[j] = layer_rows(j, core)

    def term_out(distance):
        j = row(distance)
        pair_copy(j).wait_recv()
        terms[j] += pair_in[j]

        @pl.when(j != g)
        def _():
            term_copy(j).start()

        @pl.when(j == g)
        def _():
            arrived[x, pl.ds(pl.multiple_of(core * half, half), half), :] = terms[j]

    @pl.when(r == 0)
    def _():
        for step in range(1, n_col):
            pivot_split_copy(step).start()
        for at in range(2):
            chain(1, at).start()
            chain(-1, at).start()

    for slot, step in enumerate(ORDER_OF_K[1:]):
        start(
            remote(
                uppers.at[col(step)], gathered.at[r, c], up_send.at[slot], up_recv.at[c], col=col(step)
            )
        )
    z_step(0)
    for way in (1, -1):
        start(low_copy(way))

    @pl.when((r == 0) & (g != 0))
    def _():
        row_front_copy().start()

    pivot_over_col()
    z_step(1)
    chain_hop(1)
    z_step(2)
    pivot_over_gz()
    z_step(3)
    chain_hop(2)
    z_step(4)
    pivot_out()
    z_step(5)
    chain_hop(3)
    pivot_done()
    factor_part(8)
    z_step(6)
    factor_part(8)
    chain_hop(4)
    panel_products()
    z_step(7)
    for way in (1, -1):
        low_pass(way)
    factor_part(16)
    z_step(8)
    panel_over_col()
    factor_part(16)
    z_step(9)
    factor_part(16)
    panel_over_gz()
    z_step(10)
    for way in (1, -1):
        low_far_wait(way)
    term(0)
    term(1)
    term_out(0)
    factor_part(16)
    z_step(11)
    term(-1)
    term_out(1)
    factor_part(16)
    z_step(12)
    term_out(-1)
    term(2)
    factor_part(16)
    z_step(13)
    term(-2)
    term_out(2)
    factor_part(16)
    term_out(-2)
    upper_inverse = finish_elimination(worked, product, lower_unit)

    for way in (1, -1):
        for place in range(n_col // 2):
            z_copy(way, last, place + (n_col // 2 if way > 0 else 0)).wait_recv()
    term(3)
    term(-3)
    term_out(3)
    term_out(-3)

    panel_done()
    upper = exact_dot(lower_inverse[...], row_panel[...])
    upper_panel[...] = upper
    for at in range(panels):
        span = pl.ds(at * BLOCK, BLOCK)
        lower = exact_dot(panel[at], upper_inverse)
        lower_panel[span, :] = lower
        trailing[span, :] = front[span, :] - exact_dot(lower, upper)

    for way in (1, -1):
        for place in range(n_col // 2):
            z_copy(way, last + 1, place + (0 if way > 0 else n_col // 2)).wait_recv()
    term(last + 1)
    term_out(last + 1)

    for step in range(1, n_gz):
        other = gz(step)
        span = pl.ds(pl.multiple_of(lax.rem(other, 2) * half, half), half)
        block = arrived.at[other // 2, span, :]
        remote(block, block, term_send.at[0], term_recv.at[other], gz=other).wait_recv()

    def add_up(at, carry):
        span = pl.ds(pl.multiple_of(at * BLOCK, BLOCK), BLOCK)
        total = arrived[0, span, :]
        for chip in range(1, n_gz // 2):
            total += arrived[chip, span, :]
        trailing[span, :] -= total
        return carry

    lax.fori_loop(0, panels, add_up, 0)

    for copy in sends:
        copy.wait_send()
    for step in range(1, n_gz):
        term_copy(gz(step)).wait_send()

    @pl.when(r < n_row // 2)
    def _():
        for at in range(2):
            chain(1, at).wait_send()

    @pl.when((r == 0) | (r > n_row // 2 + 1))
    def _():
        for at in range(2):
            chain(-1, at).wait_send()

    @pl.when(r == 0)
    def _():
        for step in range(1, n_col):
            pivot_split_copy(step).wait_send()
        for step in range(1, n_gz):
            pivot_sum_copy(step).wait_send()
        for step in range(1, n_row):
            pivot_row_copy(step).wait_send()

    @pl.when((r == 0) & (g != 0))
    def _():
        row_front_copy().wait_send()

    @pl.when(g != r)
    def _():
        row_copy().wait_send()

    @pl.when(g == r)
    def _():
        for step in range(1, n_row):
            spread_copy(step).wait_send()


def shards(n_gz, n_row, n_col, subtree_lower, subtree_upper, touched, front):
    height, depth = subtree_lower.shape[1:]
    width = front.shape[3]
    half = height // 2
    bf16, f32 = jnp.bfloat16, jnp.float32
    dma = pltpu.SemaphoreType.DMA
    backs = BLOCK // n_col
    vmem = pl.BlockSpec(memory_space=pltpu.VMEM)
    anywhere = pl.BlockSpec(memory_space=pltpu.HBM)
    lower_panel, upper_panel, trailing = pl.pallas_call(
        functools.partial(front_kernel, n_gz, n_row, n_col),
        out_shape=(
            jax.ShapeDtypeStruct((height, width), f32),
            jax.ShapeDtypeStruct((width, width), f32),
            jax.ShapeDtypeStruct((height, width), f32),
        ),
        in_specs=[anywhere] * 4,
        out_specs=(vmem, vmem, vmem),
        scratch_shapes=[
            pltpu.VMEM((height, depth), bf16),
            pltpu.VMEM((depth, height), bf16),
            pltpu.SMEM(touched.shape, jnp.int32),
            pltpu.VMEM((height, width), f32),
            pltpu.VMEM((n_col, height, depth), bf16),
            pltpu.VMEM((n_col, depth, BLOCK), bf16),
            pltpu.VMEM((n_row, n_col, depth, BLOCK), bf16),
            pltpu.VMEM((n_gz, half, BLOCK), f32),
            pltpu.VMEM((n_gz, half, BLOCK), f32),
            pltpu.VMEM((n_gz, half, BLOCK), f32),
            pltpu.VMEM((n_gz // 2, height, BLOCK), f32),
            pltpu.VMEM((BLOCK, depth), bf16),
            pltpu.VMEM((depth, BLOCK), bf16),
            pltpu.VMEM((BLOCK, BLOCK), f32),
            pltpu.VMEM((n_col, backs, BLOCK), f32),
            pltpu.VMEM((n_col, backs, BLOCK), f32),
            pltpu.VMEM((backs, BLOCK), f32),
            pltpu.VMEM((n_gz, backs, BLOCK), f32),
            pltpu.VMEM((n_col, backs, BLOCK), f32),
            pltpu.VMEM((n_col, 2 * BLOCK, BLOCK), f32),
            pltpu.VMEM((n_col, 2 * BLOCK, BLOCK), f32),
            pltpu.VMEM((2 * BLOCK, BLOCK), f32),
            pltpu.VMEM((n_gz, BLOCK, BLOCK), f32),
            pltpu.VMEM((n_gz, BLOCK, BLOCK), f32),
            pltpu.VMEM((n_col, BLOCK, BLOCK), f32),
            pltpu.VMEM((BLOCK, BLOCK), f32),
            pltpu.VMEM((BLOCK, BLOCK), f32),
            pltpu.VMEM((BLOCK, BLOCK), f32),
            pltpu.VMEM((BLOCK, BLOCK), f32),
            pltpu.VMEM((BLOCK, BLOCK), f32),
            dma((4,)),
            dma((n_col,)), dma((n_col,)),
            dma((4,)), dma((4,)),
            dma((2, n_row * n_col)), dma((n_row, n_col)),
            dma((n_gz,)), dma((n_gz,)),
            dma((n_gz,)), dma((n_gz,)),
            dma((2, 2)), dma((2,)),
            dma((2,)),
            dma((n_col,)), dma((n_col,)),
            dma((n_gz,)), dma((n_gz,)),
            dma((n_row,)), dma,
            dma((n_col,)), dma((n_col,)),
            dma((n_col,)), dma((n_col,)),
            dma((n_gz,)), dma((n_gz,)),
            dma, dma((n_gz,)),
            dma((n_col,)), dma((n_col,)),
            dma((n_row,)), dma,
        ],
        compiler_params=pltpu.CompilerParams(
            collective_id=0, has_side_effects=True, vmem_limit_bytes=48 * 1024 * 1024
        ),
    )(subtree_lower[0], subtree_upper[0], touched, front.reshape(height, width))
    return (
        lower_panel,
        upper_panel.reshape(width, 1, 1, width),
        trailing.reshape(height, 1, 1, width),
    )


def solution(mesh):
    placed = (
        P("gz", "row", "col"),
        P("gz", "col", "row"),
        P("gz", None),
        P("row", "gz", "col", None),
    )
    return jax.shard_map(
        functools.partial(shards, mesh.shape["gz"], mesh.shape["row"], mesh.shape["col"]),
        mesh=mesh,
        in_specs=placed,
        out_specs=(P("row", None), P(None, "gz", "col", None), P("row", "gz", "col", None)),
        check_vma=False,
    )
```

time: 110 us -> 86.6 us (0.79)
  Pallas kernels: 104 us -> 80 us
    pallas_call x1, Pallas kernels: 104 us -> 80 us  [shards(): pl.pallas_call(functools.partial(front_kernel, n_gz, n_row, n_col), out_s...]
where the time goes in v2:
time: 86.6 us; the launch traced here: 86.4 us
  Pallas kernels  80 us (92%)
  local copies, waits for them, and re-layouts  5.72 us (7%)
    pallas_call x1, Pallas kernels, shards(): pl.pallas_call(functools.partial(front_kernel, n_gz, n_row, n_col), out_s...  80 us
    unnamed x11, local copies, waits for them, and re-layouts  5.72 us

profile of v2, /device:TPU:103, one launch (start us, length us, event | category | flops | bytes accessed | tf_op | source)
XLA Modules:
  0.0 86.4 jit_solution(2590820341925260729)
XLA Ops:
  0.6 0.0 copy-start.3
  0.6 0.6 copy-done.3
  1.3 0.0 copy-start
  1.3 1.0 %copy-done = bf16[1,512,512]{2,1,0:T(8,128)(2,1)S(1)} copy-done((bf16[1,512,512]{2,1,0:T(8,128)(2,1)S(1)}, bf16[1,512,512]{2,1,0:T(8,128)(2,1)}, u32[]{:S(2)}) %copy-start) | copy-done | bytes 524312
  2.3 0.0 copy-start.1
  2.3 1.0 %copy-done.1 = bf16[1,512,512]{2,1,0:T(8,128)(2,1)S(1)} copy-done((bf16[1,512,512]{2,1,0:T(8,128)(2,1)S(1)}, bf16[1,512,512]{2,1,0:T(8,128)(2,1)}, u32[]{:S(2)}) %copy-start.1) | copy-done | bytes 524312
  3.4 0.0 copy-start.2
  3.4 0.9 %copy-done.2 = f32[512,1,1,128]{3,2,1,0:T(1,128)S(1)} copy-done((f32[512,1,1,128]{3,2,1,0:T(1,128)S(1)}, f32[512,1,1,128]{3,2,1,0:T(1,128)}, u32[]{:S(2)}) %copy-start.2) | copy-done | bytes 262168
  4.3 80.0 %shard_map.67 = (f32[512,128]{1,0:T(8,128)S(1)}, f32[128,128]{1,0:T(8,128)S(1)}, f32[512,128]{1,0:T(8,128)S(1)}) custom-call(bf16[512,512]{1,0:T(8,128)(2,1)S(1)} %bitcast.9, bf16[512,512]{1,0:T(8,128)(2,1)S(1)} %bitcast.10, s32[1,32]{1,0:T(1,128)S(1)} %copy-done.3, f32[512,128]{1,0:T(8,128)S(1)} %bitcast.11), custom_call_target="tpu_custom_call" | custom-call | tf_op jit(solution)/shard_map/pallas_call | solution.py:582
  84.3 0.7 copy.12
  85.0 0.6 copy.13
  85.7 0.7 copy.14
Async XLA Ops:
  0.6 0.7 copy-start.3
  1.3 1.0 %copy-start = (bf16[1,512,512]{2,1,0:T(8,128)(2,1)S(1)}, bf16[1,512,512]{2,1,0:T(8,128)(2,1)}, u32[]{:S(2)}) copy-start(bf16[1,512,512]{2,1,0:T(8,128)(2,1)} %param.4) | copy-start | bytes 1572868
  2.3 1.0 %copy-start.1 = (bf16[1,512,512]{2,1,0:T(8,128)(2,1)S(1)}, bf16[1,512,512]{2,1,0:T(8,128)(2,1)}, u32[]{:S(2)}) copy-start(bf16[1,512,512]{2,1,0:T(8,128)(2,1)} %param.5) | copy-start | bytes 1572868
  3.4 0.9 %copy-start.2 = (f32[512,1,1,128]{3,2,1,0:T(1,128)S(1)}, f32[512,1,1,128]{3,2,1,0:T(1,128)}, u32[]{:S(2)}) copy-start(f32[512,1,1,128]{3,2,1,0:T(1,128)} %param.7) | copy-start | bytes 786436

commit v3 on v2

--- a/solution.py
+++ b/solution.py
@@ -10,6 +10,14 @@
 BLOCK = 128
 MESH = pl.DeviceIdType.MESH
 ORDER_OF_K = (0, 1, 3, 2)
+NATURAL = [(away, place) for away in range(3) for place in range(4)] + [(3, 0), (3, 1)]
+OWN, NEXT, FAR = NATURAL[0:4], NATURAL[4:8], NATURAL[8:12]
+RING = {
+    1: OWN[:2] + NEXT + OWN[2:] + FAR + [(3, 0), (3, 1)],
+    2: OWN + FAR + NEXT + [(3, 0), (3, 1)],
+    3: OWN + NEXT[:2] + [(3, 0), (3, 1)] + NEXT[2:] + FAR,
+}
+RING_BACK = {1: RING[1], 2: RING[2], 3: OWN + NEXT + [(3, 0), (3, 1)] + FAR}
 
 
 def exact_dot(left, right):
@@ -18,7 +26,7 @@
     )
 
 
-def eliminate(first, count, worked, product, lower, lower_inverse):
+def eliminate(first, count, worked, product, upper, lower_inverse):
     rows = lax.broadcasted_iota(jnp.int32, (BLOCK, BLOCK), 0)
     lanes = lax.broadcasted_iota(jnp.int32, (BLOCK, BLOCK), 1)
 
@@ -34,26 +42,26 @@
         scaled = jnp.where(rows == at, 0.0, column / pivot)
         worked[...] = dense - scaled * pivot_row
         product[...] = product[...] - scaled * product_row
-        lower[...] = jnp.where((lanes == at) & (rows > at), scaled, lower[...])
+        upper[...] = jnp.where((lanes == at) & (rows < at), -scaled, upper[...])
         return carry
 
     lax.fori_loop(first, first + count, step, 0)
 
 
-def start_elimination(pivot, worked, product, lower):
+def start_elimination(pivot, worked, product, upper):
     rows = lax.broadcasted_iota(jnp.int32, (BLOCK, BLOCK), 0)
     lanes = lax.broadcasted_iota(jnp.int32, (BLOCK, BLOCK), 1)
     identity = jnp.where(rows == lanes, 1.0, 0.0)
     worked[...] = pivot
     product[...] = identity
-    lower[...] = identity
-
-
-def finish_elimination(worked, product, lower):
+    upper[...] = identity
+
+
+def finish_elimination(worked, upper):
     rows = lax.broadcasted_iota(jnp.int32, (BLOCK, BLOCK), 0)
     lanes = lax.broadcasted_iota(jnp.int32, (BLOCK, BLOCK), 1)
     pivots = jnp.sum(jnp.where(rows == lanes, worked[...], 0.0), axis=1, keepdims=True)
-    return exact_dot(product[...] / pivots, lower[...])
+    return upper[...] / pivots
 
 
 def remote(src, dst, send_sem, recv_sem, **where):
@@ -73,16 +81,16 @@
     lower_panel, upper_panel, trailing,
     lower_in, upper_in, touched, front,
     lowers, uppers, gathered, terms, pair_out, pair_in, arrived,
-    first_rows, first_columns, row_front,
+    first_rows, row_front,
     pivot_split, pivot_split_in, pivot_sum, pivot_sum_in, pivot,
-    split, split_in, summed, summed_in, row_in, panel, row_panel,
-    worked, product, lower_unit, lower_inverse,
+    split, split_in, summed, row_in, row_panel, column_part, column_in, panel,
+    worked, product, upper_unit, lower_inverse,
     in_sem, up_send, up_recv, low_send, low_recv, z_send, z_recv, term_send, term_recv,
     pair_send, pair_recv, chain_send, chain_recv, row_front_sem,
     pivot_split_send, pivot_split_recv, pivot_sum_send, pivot_sum_recv,
     pivot_row_send, pivot_row_recv, pivot_col_send, pivot_col_recv,
-    split_send, split_recv, summed_send, summed_recv,
-    row_send, row_recv, panel_send, panel_recv, spread_send, spread_recv,
+    split_send, split_recv, row_send, row_recv, spread_send, spread_recv,
+    column_send, column_recv, hand_send, hand_recv, panel_send, panel_recv,
 ):
     g, r, c = lax.axis_index("gz"), lax.axis_index("row"), lax.axis_index("col")
     height = lower_in.shape[0]
@@ -132,11 +140,11 @@
         lowers[c, span, :] = (lower_in[span, :].astype(jnp.float32) * mark).astype(jnp.bfloat16)
     gathered[r, c] = uppers[c]
     corner = (g == 0) & (c == 0)
+    strip = height // n_gz
 
     @pl.when(r == 0)
     def _():
         first_rows[...] = lowers[c, :BLOCK, :]
-        first_columns[...] = uppers[0]
         part = -jnp.dot(lowers[c, :BLOCK, :], uppers[0], preferred_element_type=jnp.float32)
         for at in range(n_col):
             pivot_split[at] = part[at * backs : (at + 1) * backs]
@@ -213,12 +221,12 @@
                 piece, piece, pivot_col_send.at[0], pivot_col_recv.at[col(step)], col=col(step)
             ).wait_recv()
         whole = jnp.concatenate([pivot[at] for at in range(n_col)], axis=0)
-        start_elimination(whole, worked, product, lower_unit)
+        start_elimination(whole, worked, product, upper_unit)
 
     def chain(way, at):
         slot = 0 if way > 0 else 1
-        buffer = (first_columns, first_rows)[at]
-        return remote(buffer, buffer, chain_send.at[slot, at], chain_recv.at[at], row=row(way))
+        piece = first_rows.at[pl.ds(at * (BLOCK // 2), BLOCK // 2), :]
+        return remote(piece, piece, chain_send.at[slot, at], chain_recv.at[at], row=row(way))
 
     def chain_hop(hop):
         def pass_on(way):
@@ -246,30 +254,52 @@
             uppers.at[0], gathered.at[r, col(step)], up_send.at[0], up_recv.at[col(step)], col=col(step)
         ).wait_recv()
 
-    def z_copy(way, distance, place):
-        source = row(-way * distance)
+    def z_wait(source, place):
         k_block = col(ORDER_OF_K[place])
         piece = gathered.at[source, k_block]
-        slot = 0 if way > 0 else 1
-        at = distance * n_col + place
-        return remote(piece, piece, z_send.at[slot, at], z_recv.at[source, k_block], row=row(way))
+        remote(piece, piece, z_send.at[0, 0], z_recv.at[source, k_block], row=row(1)).wait_recv()
 
     last = n_row // 2 - 1
-    z_order = [(distance, place) for distance in range(last) for place in range(n_col)]
-    z_order += [(last, place) for place in range(n_col // 2)]
+
+    def ring_entry(way, at):
+        def entry(order):
+            away, place = order[at]
+            if away == last and way < 0:
+                place += n_col // 2
+            return away, ORDER_OF_K[place]
+
+        from_first = r if way > 0 else lax.rem(n_row - r, n_row)
+        away, offset = entry(NATURAL)
+        if all(entry(order) == (away, offset) for order in (RING if way > 0 else RING_BACK).values()):
+            return away, offset
+        for distance, order in (RING if way > 0 else RING_BACK).items():
+            here = from_first == distance
+            away = jnp.where(here, entry(order)[0], away)
+            offset = jnp.where(here, entry(order)[1], offset)
+        return away, offset
 
     def z_step(at):
-        distance, place = z_order[at]
-        if distance == 0 and place > 0:
-            up_arrive(ORDER_OF_K[place])
+        if 0 < at < n_col:
+            up_arrive(ORDER_OF_K[at])
         for way in (1, -1):
-            used = place
-            if distance == last and way < 0:
-                used = place + n_col // 2
-            copy = z_copy(way, distance, used)
-            if distance > 0:
+            away, offset = ring_entry(way, at)
+            source, k_block = row(-way * away), col(offset)
+            piece = gathered.at[source, k_block]
+            slot = 0 if way > 0 else 1
+            copy = remote(piece, piece, z_send.at[slot, at], z_recv.at[source, k_block], row=row(way))
+            if not isinstance(away, int):
+                pl.when(away > 0)(copy.wait_recv)
+            elif away > 0:
                 copy.wait_recv()
             start(copy)
+
+    def far_wait(distance, way, places):
+        source = row(-way * distance)
+
+        @pl.when(source != 0)
+        def _():
+            for place in places:
+                z_wait(source, place)
 
     def low_copy(way):
         slot = 0 if way > 0 else 1
@@ -289,21 +319,9 @@
         piece = lowers.at[col(2), pl.ds(slot * half, half), :]
         remote(piece, piece, low_send.at[2 + slot], low_recv.at[2 + slot], col=col(way)).wait_recv()
 
-    def panel_products():
-        column = first_columns[...]
+    def row_products():
         for at in range(n_col):
-            split[at, :BLOCK] = -jnp.dot(
-                lowers[c, at * BLOCK : (at + 1) * BLOCK, :], column, preferred_element_type=jnp.float32
-            )
-            split[at, BLOCK:] = -jnp.dot(
-                first_rows[...], uppers[at], preferred_element_type=jnp.float32
-            )
-
-        @pl.when(corner)
-        def _():
-            for at in range(n_col):
-                split[at, :BLOCK] += front[at * BLOCK : (at + 1) * BLOCK, :]
-
+            split[at] = -jnp.dot(first_rows[...], uppers[at], preferred_element_type=jnp.float32)
         for step in range(1, n_col):
             start(
                 remote(
@@ -313,9 +331,9 @@
             )
 
     def row_copy():
-        return remote(summed.at[pl.ds(BLOCK, BLOCK), :], row_in.at[g], row_send, row_recv.at[g], gz=r)
-
-    def panel_over_col():
+        return remote(summed, row_in.at[g], row_send, row_recv.at[g], gz=r)
+
+    def row_over_col():
         for step in range(1, n_col):
             remote(
                 split.at[0], split_in.at[col(step)],
@@ -330,52 +348,86 @@
         def _():
             row_copy().start()
 
-        for step in range(1, n_gz):
-            start(
-                remote(
-                    summed.at[pl.ds(0, BLOCK), :], summed_in.at[g],
-                    summed_send.at[step], summed_recv.at[g], gz=gz(step),
-                )
-            )
-
     def spread_copy(step):
         return remote(row_panel, row_panel, spread_send.at[step], spread_recv, row=row(step))
 
-    def panel_over_gz():
+    def row_over_gz():
         @pl.when(g == r)
         def _():
             @pl.when(g != 0)
             def _():
                 row_front_copy().wait_recv()
 
-            total = summed[BLOCK:, :] + row_front[...]
+            total = summed[...] + row_front[...]
             for step in range(1, n_gz):
                 remote(
-                    summed.at[pl.ds(BLOCK, BLOCK), :], row_in.at[gz(step)],
-                    row_send, row_recv.at[gz(step)], gz=gz(step),
+                    summed, row_in.at[gz(step)], row_send, row_recv.at[gz(step)], gz=gz(step)
                 ).wait_recv()
                 total += row_in[gz(step)]
             row_panel[...] = total
             for step in range(1, n_row):
                 spread_copy(step).start()
 
-        total = summed[:BLOCK, :]
+    def strip_of(at):
+        return pl.ds(pl.multiple_of(at * strip, strip), strip)
+
+    def column_copy(step):
+        return remote(
+            column_part.at[strip_of(gz(step)), :], column_in.at[g],
+            column_send.at[step], column_recv.at[g], gz=gz(step),
+        )
+
+    def hand_copy(step):
+        piece = panel.at[strip_of(g), :]
+        return remote(piece, piece, hand_send.at[step], hand_recv, col=col(step))
+
+    def column_product():
+        far = n_row // 2
+        for plane, places in ((far - 1, (2, 3)), (far, (0, 1, 2, 3)), (far + 1, (0, 1))):
+            @pl.when(r == plane)
+            def _():
+                for place in places:
+                    z_wait(0, place)
+
+        @pl.when(c == 0)
+        def _():
+            for which in range(2):
+                column_part[which * half : (which + 1) * half, :] = -layer_rows(0, which)
+
+            @pl.when(g == 0)
+            def _():
+                column_part[...] += front[...]
+
+            for step in range(1, n_gz):
+                column_copy(step).start()
+
+    def column_over_gz():
+        @pl.when(c == 0)
+        def _():
+            total = column_part[strip_of(g), :]
+            for step in range(1, n_gz):
+                remote(
+                    column_part.at[strip_of(g), :], column_in.at[gz(step)],
+                    column_send.at[0], column_recv.at[gz(step)], gz=gz(step),
+                ).wait_recv()
+                total += column_in[gz(step)]
+            panel[strip_of(g), :] = total
+            for step in range(1, n_col):
+                hand_copy(step).start()
+
+    def column_gather():
+        @pl.when(c != 0)
+        def _():
+            hand_copy(1).wait_recv()
+
+        piece = panel.at[strip_of(g), :]
         for step in range(1, n_gz):
-            remote(
-                summed.at[pl.ds(0, BLOCK), :], summed_in.at[gz(step)],
-                summed_send.at[0], summed_recv.at[gz(step)], gz=gz(step),
-            ).wait_recv()
-            total += summed_in[gz(step)]
-        panel[c] = total
-        for step in range(1, n_col):
-            start(
-                remote(panel.at[c], panel.at[c], panel_send.at[step], panel_recv.at[c], col=col(step))
-            )
+            start(remote(piece, piece, panel_send.at[step], panel_recv.at[g], gz=gz(step)))
 
     def panel_done():
-        for step in range(1, n_col):
-            piece = panel.at[col(step)]
-            remote(piece, piece, panel_send.at[0], panel_recv.at[col(step)], col=col(step)).wait_recv()
+        for step in range(1, n_gz):
+            piece = panel.at[strip_of(gz(step)), :]
+            remote(piece, piece, panel_send.at[0], panel_recv.at[gz(step)], gz=gz(step)).wait_recv()
 
         @pl.when(g != r)
         def _():
@@ -384,7 +436,7 @@
     done = [0]
 
     def factor_part(count):
-        eliminate(done[0], count, worked, product, lower_unit, lower_inverse)
+        eliminate(done[0], count, worked, product, upper_unit, lower_inverse)
         done[0] += count
 
     def term_copy(j):
@@ -392,7 +444,9 @@
         return remote(terms.at[j], arrived.at[x, span, :], term_send.at[j], term_recv.at[g], gz=j)
 
     def layer_rows(j, which):
-        span = pl.ds(pl.multiple_of(which * half, half), half)
+        span = pl.ds(which * half, half)
+        if not isinstance(which, int):
+            span = pl.ds(pl.multiple_of(which * half, half), half)
         total = jnp.dot(lowers[0, span, :], gathered[j, 0], preferred_element_type=jnp.float32)
         for k_block in range(1, n_col):
             total += jnp.dot(
@@ -405,22 +459,28 @@
 
     def term(distance):
         j = row(distance)
-        pair_out[j] = layer_rows(j, 1 - core)
-        start(pair_copy(j))
-        terms[j] = layer_rows(j, core)
+
+        @pl.when((j != 0) | (c != 0))
+        def _():
+            pair_out[j] = layer_rows(j, 1 - core)
+            pair_copy(j).start()
+            terms[j] = layer_rows(j, core)
 
     def term_out(distance):
         j = row(distance)
-        pair_copy(j).wait_recv()
-        terms[j] += pair_in[j]
-
-        @pl.when(j != g)
-        def _():
-            term_copy(j).start()
-
-        @pl.when(j == g)
-        def _():
-            arrived[x, pl.ds(pl.multiple_of(core * half, half), half), :] = terms[j]
+
+        @pl.when((j != 0) | (c != 0))
+        def _():
+            pair_copy(j).wait_recv()
+            terms[j] += pair_in[j]
+
+            @pl.when(j != g)
+            def _():
+                term_copy(j).start()
+
+            @pl.when(j == g)
+            def _():
+                arrived[x, pl.ds(pl.multiple_of(core * half, half), half), :] = terms[j]
 
     @pl.when(r == 0)
     def _():
@@ -444,6 +504,21 @@
     def _():
         row_front_copy().start()
 
+    def panels_out(upper_inverse):
+        panel_done()
+        upper = exact_dot(lower_inverse[...], row_panel[...])
+        upper_panel[...] = upper
+        for at in range(panels):
+            span = pl.ds(at * BLOCK, BLOCK)
+            lower = exact_dot(panel[span, :], upper_inverse)
+            lower_panel[span, :] = lower
+            kept = jnp.where(corner, panel[span, :], front[span, :])
+            trailing[span, :] = kept - exact_dot(lower, upper)
+
+    def far_arrive():
+        far_wait(last + 1, 1, (0, 1))
+        far_wait(last + 1, -1, (2, 3))
+
     pivot_over_col()
     z_step(1)
     chain_hop(1)
@@ -453,89 +528,94 @@
     chain_hop(2)
     z_step(4)
     pivot_out()
+    chain_hop(3)
     z_step(5)
-    chain_hop(3)
     pivot_done()
     factor_part(8)
+    chain_hop(4)
+    row_products()
+    factor_part(8)
     z_step(6)
-    factor_part(8)
-    chain_hop(4)
-    panel_products()
-    z_step(7)
     for way in (1, -1):
         low_pass(way)
+    factor_part(8)
+    z_step(7)
+    row_over_col()
     factor_part(16)
     z_step(8)
-    panel_over_col()
     factor_part(16)
     z_step(9)
+    row_over_gz()
     factor_part(16)
-    panel_over_gz()
     z_step(10)
+    factor_part(8)
+    z_step(11)
     for way in (1, -1):
         low_far_wait(way)
     term(0)
     term(1)
+    column_product()
+    term(-1)
     term_out(0)
-    factor_part(16)
-    z_step(11)
-    term(-1)
     term_out(1)
-    factor_part(16)
     z_step(12)
+    factor_part(8)
     term_out(-1)
+    column_over_gz()
+    z_step(13)
     term(2)
-    factor_part(16)
-    z_step(13)
+    column_gather()
     term(-2)
     term_out(2)
-    factor_part(16)
     term_out(-2)
-    upper_inverse = finish_elimination(worked, product, lower_unit)
-
-    for way in (1, -1):
-        for place in range(n_col // 2):
-            z_copy(way, last, place + (n_col // 2 if way > 0 else 0)).wait_recv()
+    far_wait(last, 1, (2, 3))
+    far_wait(last, -1, (0, 1))
     term(3)
     term(-3)
     term_out(3)
     term_out(-3)
-
-    panel_done()
-    upper = exact_dot(lower_inverse[...], row_panel[...])
-    upper_panel[...] = upper
-    for at in range(panels):
-        span = pl.ds(at * BLOCK, BLOCK)
-        lower = exact_dot(panel[at], upper_inverse)
-        lower_panel[span, :] = lower
-        trailing[span, :] = front[span, :] - exact_dot(lower, upper)
-
-    for way in (1, -1):
-        for place in range(n_col // 2):
-            z_copy(way, last + 1, place + (0 if way > 0 else n_col // 2)).wait_recv()
-    term(last + 1)
-    term_out(last + 1)
-
-    for step in range(1, n_gz):
-        other = gz(step)
-        span = pl.ds(pl.multiple_of(lax.rem(other, 2) * half, half), half)
-        block = arrived.at[other // 2, span, :]
-        remote(block, block, term_send.at[0], term_recv.at[other], gz=other).wait_recv()
-
-    def add_up(at, carry):
-        span = pl.ds(pl.multiple_of(at * BLOCK, BLOCK), BLOCK)
-        total = arrived[0, span, :]
-        for chip in range(1, n_gz // 2):
-            total += arrived[chip, span, :]
-        trailing[span, :] -= total
-        return carry
-
-    lax.fori_loop(0, panels, add_up, 0)
+    far_arrive()
+    term(4)
+    term_out(4)
+    factor_part(40)
+    upper_inverse = finish_elimination(worked, upper_unit)
+    panels_out(upper_inverse)
+
+    @pl.when((g != 0) | (c != 0))
+    def _():
+        for step in range(1, n_gz):
+            other = gz(step)
+            span = pl.ds(pl.multiple_of(lax.rem(other, 2) * half, half), half)
+            block = arrived.at[other // 2, span, :]
+            remote(block, block, term_send.at[0], term_recv.at[other], gz=other).wait_recv()
+
+        def add_up(at, carry):
+            span = pl.ds(pl.multiple_of(at * BLOCK, BLOCK), BLOCK)
+            total = arrived[0, span, :]
+            for chip in range(1, n_gz // 2):
+                total += arrived[chip, span, :]
+            trailing[span, :] -= total
+            return carry
+
+        lax.fori_loop(0, panels, add_up, 0)
 
     for copy in sends:
         copy.wait_send()
-    for step in range(1, n_gz):
-        term_copy(gz(step)).wait_send()
+    for step in range(n_gz):
+        j = gz(step)
+
+        @pl.when((j != 0) | (c != 0))
+        def _():
+            pair_copy(j).wait_send()
+            if step:
+                term_copy(j).wait_send()
+
+    @pl.when(c == 0)
+    def _():
+        for step in range(1, n_gz):
+            column_copy(step).wait_send()
+        for step in range(1, n_col):
+            hand_copy(step).wait_send()
 
     @pl.when(r < n_row // 2)
     def _():
@@ -601,20 +681,20 @@
             pltpu.VMEM((n_gz, half, BLOCK), f32),
             pltpu.VMEM((n_gz // 2, height, BLOCK), f32),
             pltpu.VMEM((BLOCK, depth), bf16),
-            pltpu.VMEM((depth, BLOCK), bf16),
             pltpu.VMEM((BLOCK, BLOCK), f32),
             pltpu.VMEM((n_col, backs, BLOCK), f32),
             pltpu.VMEM((n_col, backs, BLOCK), f32),
             pltpu.VMEM((backs, BLOCK), f32),
             pltpu.VMEM((n_gz, backs, BLOCK), f32),
             pltpu.VMEM((n_col, backs, BLOCK), f32),
-            pltpu.VMEM((n_col, 2 * BLOCK, BLOCK), f32),
-            pltpu.VMEM((n_col, 2 * BLOCK, BLOCK), f32),
-            pltpu.VMEM((2 * BLOCK, BLOCK), f32),
-            pltpu.VMEM((n_gz, BLOCK, BLOCK), f32),
-            pltpu.VMEM((n_gz, BLOCK, BLOCK), f32),
+            pltpu.VMEM((n_col, BLOCK, BLOCK), f32),
             pltpu.VMEM((n_col, BLOCK, BLOCK), f32),
             pltpu.VMEM((BLOCK, BLOCK), f32),
+            pltpu.VMEM((n_gz, BLOCK, BLOCK), f32),
+            pltpu.VMEM((BLOCK, BLOCK), f32),
+            pltpu.VMEM((height, BLOCK), f32),
+            pltpu.VMEM((n_gz, height // n_gz, BLOCK), f32),
+            pltpu.VMEM((height, BLOCK), f32),
             pltpu.VMEM((BLOCK, BLOCK), f32),
             pltpu.VMEM((BLOCK, BLOCK), f32),
             pltpu.VMEM((BLOCK, BLOCK), f32),
@@ -622,7 +702,7 @@
             dma((4,)),
             dma((n_col,)), dma((n_col,)),
             dma((4,)), dma((4,)),
-            dma((2, n_row * n_col)), dma((n_row, n_col)),
+            dma((2, len(NATURAL))), dma((n_row, n_col)),
             dma((n_gz,)), dma((n_gz,)),
             dma((n_gz,)), dma((n_gz,)),
             dma((2, 2)), dma((2,)),
@@ -632,13 +712,14 @@
             dma((n_row,)), dma,
             dma((n_col,)), dma((n_col,)),
             dma((n_col,)), dma((n_col,)),
+            dma, dma((n_gz,)),
+            dma((n_row,)), dma,
             dma((n_gz,)), dma((n_gz,)),
-            dma, dma((n_gz,)),
-            dma((n_col,)), dma((n_col,)),
-            dma((n_row,)), dma,
+            dma((n_col,)), dma,
+            dma((n_gz,)), dma((n_gz,)),
         ],
         compiler_params=pltpu.CompilerParams(
-            collective_id=0, has_side_effects=True, vmem_limit_bytes=48 * 1024 * 1024
+            collective_id=0, has_side_effects=True, vmem_limit_bytes=63 * 1024 * 1024
         ),
     )(subtree_lower[0], subtree_upper[0], touched, front.reshape(height, width))
     return (

time: 86.6 us -> 80.1 us (0.925)
  the two profiles are of different devices: /device:TPU:103 before, /device:TPU:144 now
where the time goes in v3:
time: 80.1 us; the launch traced here: 79.7 us
  Pallas kernels  76 us (95%)
  local copies, waits for them, and re-layouts  3.06 us (4%)
    pallas_call x1, Pallas kernels, shards(): pl.pallas_call(functools.partial(front_kernel, n_gz, n_row, n_col), out_s...  76 us
    unnamed x7, local copies, waits for them, and re-layouts  3.06 us

profile of v3, /device:TPU:144, one launch (start us, length us, event | category | flops | bytes accessed | tf_op | source)
XLA Modules:
  0.0 79.7 jit_solution(11007212315847592055)
XLA Ops:
  0.6 76.0 %shard_map.67 = (f32[512,128]{1,0:T(8,128)}, f32[128,128]{1,0:T(8,128)}, f32[512,128]{1,0:T(8,128)}) custom-call(bf16[512,512]{1,0:T(8,128)(2,1)} %bitcast.9, bf16[512,512]{1,0:T(8,128)(2,1)} %bitcast.10, s32[1,32]{1,0:T(1,128)} %touched_hbm.1, f32[512,128]{1,0:T(8,128)} %bitcast.11), custom_call_target="tpu_custom_call" | custom-call | tf_op jit(solution)/shard_map/pallas_call | solution.py:662
  76.7 0.0 copy-start.1
  76.7 0.0 copy-start
  76.7 1.7 %copy.12 = f32[512,128]{1,0:T(8,128)} copy(f32[512,128]{1,0:T(8,128)} %get-tuple-element.15) | data formatting | bytes 524288
  78.4 0.0 copy-done.1
  78.4 0.6 copy.13
  79.0 0.0 copy-done
  79.0 0.7 copy.14
Async XLA Ops:
  76.7 1.7 %copy-start.1 = (f32[128,128]{1,0:T(8,128)S(1)}, f32[128,128]{1,0:T(8,128)}, u32[]{:S(2)}) copy-start(f32[128,128]{1,0:T(8,128)} %get-tuple-element.7) | copy-start | bytes 196612
  76.7 2.4 %copy-start = (f32[512,128]{1,0:T(8,128)S(1)}, f32[512,128]{1,0:T(8,128)}, u32[]{:S(2)}) copy-start(f32[512,128]{1,0:T(8,128)} %get-tuple-element.8) | copy-start | bytes 786436

commit v4 on v3

--- a/solution.py
+++ b/solution.py
@@ -8,6 +8,7 @@
 from jax.sharding import PartitionSpec as P
 
 BLOCK = 128
+GROUP = 4
 MESH = pl.DeviceIdType.MESH
 ORDER_OF_K = (0, 1, 3, 2)
 NATURAL = [(away, place) for away in range(3) for place in range(4)] + [(3, 0), (3, 1)]
@@ -27,25 +28,45 @@
 
 
 def eliminate(first, count, worked, product, upper, lower_inverse):
-    rows = lax.broadcasted_iota(jnp.int32, (BLOCK, BLOCK), 0)
-    lanes = lax.broadcasted_iota(jnp.int32, (BLOCK, BLOCK), 1)
-
-    def step(at, carry):
-        dense = worked[...]
-        pivot_row = worked[pl.ds(at, 1), :]
-        product_row = product[pl.ds(at, 1), :]
-        lower_inverse[pl.ds(at, 1), :] = product_row
-        column = jnp.sum(jnp.where(lanes == at, dense, 0.0), axis=1, keepdims=True)
-        pivot = jnp.sum(
-            jnp.where(lanes[:1] == at, pivot_row, 0.0), axis=1, keepdims=True
-        )
-        scaled = jnp.where(rows == at, 0.0, column / pivot)
-        worked[...] = dense - scaled * pivot_row
-        product[...] = product[...] - scaled * product_row
-        upper[...] = jnp.where((lanes == at) & (rows < at), -scaled, upper[...])
+    lanes = lax.broadcasted_iota(jnp.int32, (1, BLOCK), 1)
+    rows = lax.broadcasted_iota(jnp.int32, (BLOCK, 1), 0)
+
+    def step(group, carry):
+        places = [group * GROUP + s for s in range(GROUP)]
+        here = [lanes == place for place in places]
+        dense, products, kept = worked[...], product[...], upper[...]
+        pivot_rows = [worked[pl.ds(place, 1), :] for place in places]
+        product_rows = [product[pl.ds(place, 1), :] for place in places]
+
+        def take(values, hit):
+            return jnp.sum(jnp.where(hit, values, 0.0), axis=1, keepdims=True)
+
+        columns = [take(dense, hit) for hit in here]
+        corner = [[take(line, hit) for hit in here] for line in pivot_rows]
+        scaled = []
+        for s in range(GROUP):
+            inverse = 1.0 / corner[s][s]
+            factors = jnp.where(rows == places[s], 0.0, columns[s] * inverse)
+            for u in range(s + 1, GROUP):
+                ratio = corner[u][s] * inverse
+                pivot_rows[u] = pivot_rows[u] - ratio * pivot_rows[s]
+                product_rows[u] = product_rows[u] - ratio * product_rows[s]
+                for t in range(s + 1, GROUP):
+                    corner[u][t] = corner[u][t] - ratio * corner[s][t]
+            for t in range(s + 1, GROUP):
+                columns[t] = columns[t] - factors * corner[s][t]
+            scaled.append(factors)
+        for s in range(GROUP):
+            lower_inverse[pl.ds(places[s], 1), :] = product_rows[s]
+            dense = dense - scaled[s] * pivot_rows[s]
+            products = products - scaled[s] * product_rows[s]
+            kept = jnp.where(here[s], -scaled[s], kept)
+        worked[...] = dense
+        product[...] = products
+        upper[...] = kept
         return carry
 
-    lax.fori_loop(first, first + count, step, 0)
+    lax.fori_loop(first // GROUP, (first + count) // GROUP, step, 0)
 
 
 def start_elimination(pivot, worked, product, upper):
@@ -61,7 +82,8 @@
     rows = lax.broadcasted_iota(jnp.int32, (BLOCK, BLOCK), 0)
     lanes = lax.broadcasted_iota(jnp.int32, (BLOCK, BLOCK), 1)
     pivots = jnp.sum(jnp.where(rows == lanes, worked[...], 0.0), axis=1, keepdims=True)
-    return upper[...] / pivots
+    unit = jnp.where(rows < lanes, upper[...], jnp.where(rows == lanes, 1.0, 0.0))
+    return unit / pivots
 
 
 def remote(src, dst, send_sem, recv_sem, **where):
@@ -138,7 +160,7 @@
         span = pl.ds(at * BLOCK, BLOCK)
         uppers[at] = (upper_in[:, span].astype(jnp.float32) * mark).astype(jnp.bfloat16)
         lowers[c, span, :] = (lower_in[span, :].astype(jnp.float32) * mark).astype(jnp.bfloat16)
-    gathered[r, c] = uppers[c]
+    gathered[0, c, :, :BLOCK] = uppers[c]
     corner = (g == 0) & (c == 0)
     strip = height // n_gz
 
@@ -249,15 +271,20 @@
             front.at[pl.ds(0, BLOCK), :], row_front, row_front_sem.at[0], row_front_sem.at[1], row=g
         )
 
+    def side(way):
+        return pl.ds(0 if way > 0 else BLOCK, BLOCK)
+
     def up_arrive(step):
+        block = gathered.at[0, col(step), :, side(1)]
+        remote(uppers.at[0], block, up_send.at[0], up_recv.at[col(step)], col=col(step)).wait_recv()
+
+    def z_wait(distance, way, place):
+        k_block = col(ORDER_OF_K[place])
+        slot = 0 if way > 0 else 1
+        piece = gathered.at[distance, k_block, :, side(way)]
         remote(
-            uppers.at[0], gathered.at[r, col(step)], up_send.at[0], up_recv.at[col(step)], col=col(step)
+            piece, piece, z_send.at[0, 0], z_recv.at[distance, slot, k_block], row=row(1)
         ).wait_recv()
-
-    def z_wait(source, place):
-        k_block = col(ORDER_OF_K[place])
-        piece = gathered.at[source, k_block]
-        remote(piece, piece, z_send.at[0, 0], z_recv.at[source, k_block], row=row(1)).wait_recv()
 
     last = n_row // 2 - 1
 
@@ -283,41 +310,59 @@
             up_arrive(ORDER_OF_K[at])
         for way in (1, -1):
             away, offset = ring_entry(way, at)
-            source, k_block = row(-way * away), col(offset)
-            piece = gathered.at[source, k_block]
+            k_block = col(offset)
             slot = 0 if way > 0 else 1
-            copy = remote(piece, piece, z_send.at[slot, at], z_recv.at[source, k_block], row=row(way))
+            lanes = side(way)
+            if way < 0:
+                start_lane = jnp.where(away == 0, 0, BLOCK)
+                lanes = pl.ds(pl.multiple_of(start_lane, BLOCK), BLOCK)
+            copy = remote(
+                gathered.at[away, k_block, :, lanes], gathered.at[away + 1, k_block, :, side(way)],
+                z_send.at[slot, at], z_recv.at[away + 1, slot, k_block], row=row(way),
+            )
+            arrived_here = gathered.at[away, k_block, :, lanes]
+            arrival = remote(
+                arrived_here, arrived_here, z_send.at[slot, at], z_recv.at[away, slot, k_block], row=row(way)
+            )
             if not isinstance(away, int):
-                pl.when(away > 0)(copy.wait_recv)
+                pl.when(away > 0)(arrival.wait_recv)
             elif away > 0:
-                copy.wait_recv()
+                arrival.wait_recv()
             start(copy)
 
     def far_wait(distance, way, places):
-        source = row(-way * distance)
-
-        @pl.when(source != 0)
+        @pl.when(row(-way * distance) != 0)
         def _():
             for place in places:
-                z_wait(source, place)
-
-    def low_copy(way):
+                z_wait(distance, way, place)
+
+    def half_of(at):
+        return pl.ds(at * half, half)
+
+    def low_copy(way, second):
         slot = 0 if way > 0 else 1
-        return remote(
-            lowers.at[c], lowers.at[c], low_send.at[slot], low_recv.at[slot], col=col(way)
-        )
-
-    def low_pass(way):
-        slot = 0 if way > 0 else 1
-        block = lowers.at[col(-way)]
-        remote(block, block, low_send.at[slot], low_recv.at[slot], col=col(way)).wait_recv()
-        piece = lowers.at[col(-way), pl.ds(slot * half, half), :]
-        start(remote(piece, piece, low_send.at[2 + slot], low_recv.at[2 + slot], col=col(way)))
-
-    def low_far_wait(way):
-        slot = 0 if way > 0 else 1
-        piece = lowers.at[col(2), pl.ds(slot * half, half), :]
-        remote(piece, piece, low_send.at[2 + slot], low_recv.at[2 + slot], col=col(way)).wait_recv()
+        piece = lowers.at[c, half_of(1 - slot if second else slot), :]
+        at = 4 + slot if second else slot
+        return remote(piece, piece, low_send.at[at], low_recv.at[at], col=col(way))
+
+    def low_start(second):
+        for way in (1, -1):
+            start(low_copy(way, second))
+
+    def low_pass():
+        for way in (1, -1):
+            slot = 0 if way > 0 else 1
+            piece = lowers.at[col(-way), half_of(slot), :]
+            remote(piece, piece, low_send.at[slot], low_recv.at[slot], col=col(way)).wait_recv()
+            start(remote(piece, piece, low_send.at[2 + slot], low_recv.at[2 + slot], col=col(way)))
+
+    def low_done():
+        for way in (1, -1):
+            slot = 0 if way > 0 else 1
+            piece = lowers.at[col(-way), half_of(1 - slot), :]
+            remote(piece, piece, low_send.at[4 + slot], low_recv.at[4 + slot], col=col(way)).wait_recv()
+            piece = lowers.at[col(2), half_of(slot), :]
+            remote(piece, piece, low_send.at[2 + slot], low_recv.at[2 + slot], col=col(way)).wait_recv()
 
     def row_products():
         for at in range(n_col):
@@ -383,16 +428,27 @@
 
     def column_product():
         far = n_row // 2
-        for plane, places in ((far - 1, (2, 3)), (far, (0, 1, 2, 3)), (far + 1, (0, 1))):
+        for plane, waits in (
+            (far - 1, ((1, 2), (1, 3))),
+            (far, ((1, 0), (1, 1), (-1, 2), (-1, 3))),
+            (far + 1, ((-1, 0), (-1, 1))),
+        ):
             @pl.when(r == plane)
             def _():
-                for place in places:
-                    z_wait(0, place)
+                for way, place in waits:
+                    z_wait(min(plane, n_row - plane), way, place)
+
+        distance = jnp.where(r <= far, r, n_row - r)
+
+        def first_block(place):
+            up = (r < far) | ((r == far) & (place < 2))
+            lanes = pl.ds(pl.multiple_of(jnp.where(up, 0, BLOCK), BLOCK), BLOCK)
+            return gathered[distance, col(ORDER_OF_K[place]), :, lanes]
 
         @pl.when(c == 0)
         def _():
             for which in range(2):
-                column_part[which * half : (which + 1) * half, :] = -layer_rows(0, which)
+                column_part[which * half : (which + 1) * half, :] = -layer_rows(first_block, which)
 
             @pl.when(g == 0)
             def _():
@@ -443,28 +499,39 @@
         span = pl.ds(pl.multiple_of(core * half, half), half)
         return remote(terms.at[j], arrived.at[x, span, :], term_send.at[j], term_recv.at[g], gz=j)
 
-    def layer_rows(j, which):
+    def layer_rows(block, which):
         span = pl.ds(which * half, half)
         if not isinstance(which, int):
             span = pl.ds(pl.multiple_of(which * half, half), half)
-        total = jnp.dot(lowers[0, span, :], gathered[j, 0], preferred_element_type=jnp.float32)
-        for k_block in range(1, n_col):
-            total += jnp.dot(
-                lowers[k_block, span, :], gathered[j, k_block], preferred_element_type=jnp.float32
-            )
+        total = None
+        for place in range(n_col):
+            k_block = col(ORDER_OF_K[place])
+            part = jnp.dot(lowers[k_block, span, :], block(place), preferred_element_type=jnp.float32)
+            total = part if total is None else total + part
         return total
 
     def pair_copy(j):
         return remote(pair_out.at[j], pair_in.at[j], pair_send.at[j], pair_recv.at[j], gz=sibling)
 
     def term(distance):
-        j = row(distance)
-
-        @pl.when((j != 0) | (c != 0))
-        def _():
-            pair_out[j] = layer_rows(j, 1 - core)
-            pair_copy(j).start()
-            terms[j] = layer_rows(j, core)
+        def block(place):
+            k_block = col(ORDER_OF_K[place])
+            if 0 < distance <= last:
+                return gathered[distance, k_block]
+            return gathered[distance, k_block, :, side(1 if distance == 0 or place < 2 else -1)]
+
+        ends = (row(-distance), row(distance)) if 0 < distance <= last else (row(distance),)
+
+        def put(where, values, send):
+            for at, j in enumerate(ends):
+                @pl.when((j != 0) | (c != 0))
+                def _():
+                    where[j] = values[:, at * BLOCK : (at + 1) * BLOCK]
+                    if send:
+                        pair_copy(j).start()
+
+        put(pair_out, layer_rows(block, 1 - core), True)
+        put(terms, layer_rows(block, core), False)
 
     def term_out(distance):
         j = row(distance)
@@ -491,14 +558,10 @@
             chain(-1, at).start()
 
     for slot, step in enumerate(ORDER_OF_K[1:]):
-        start(
-            remote(
-                uppers.at[col(step)], gathered.at[r, c], up_send.at[slot], up_recv.at[c], col=col(step)
-            )
-        )
+        mine = gathered.at[0, c, :, side(1)]
+        start(remote(uppers.at[col(step)], mine, up_send.at[slot], up_recv.at[c], col=col(step)))
     z_step(0)
-    for way in (1, -1):
-        start(low_copy(way))
+    low_start(False)
 
     @pl.when((r == 0) & (g != 0))
     def _():
@@ -523,11 +586,13 @@
     z_step(1)
     chain_hop(1)
     z_step(2)
+    low_start(True)
     pivot_over_gz()
     z_step(3)
     chain_hop(2)
     z_step(4)
     pivot_out()
+    low_pass()
     chain_hop(3)
     z_step(5)
     pivot_done()
@@ -536,8 +601,6 @@
     row_products()
     factor_part(8)
     z_step(6)
-    for way in (1, -1):
-        low_pass(way)
     factor_part(8)
     z_step(7)
     row_over_col()
@@ -546,32 +609,28 @@
     factor_part(16)
     z_step(9)
     row_over_gz()
+    low_done()
+    term(0)
+    factor_part(8)
+    z_step(10)
+    column_product()
+    term_out(0)
     factor_part(16)
-    z_step(10)
+    z_step(11)
+    term(1)
+    column_over_gz()
+    term_out(1)
+    term_out(-1)
+    z_step(12)
+    column_gather()
     factor_part(8)
-    z_step(11)
-    for way in (1, -1):
-        low_far_wait(way)
-    term(0)
-    term(1)
-    column_product()
-    term(-1)
-    term_out(0)
-    term_out(1)
-    z_step(12)
-    factor_part(8)
-    term_out(-1)
-    column_over_gz()
     z_step(13)
     term(2)
-    column_gather()
-    term(-2)
     term_out(2)
     term_out(-2)
     far_wait(last, 1, (2, 3))
     far_wait(last, -1, (0, 1))
     term(3)
-    term(-3)
     term_out(3)
     term_out(-3)
     far_arrive()
@@ -675,7 +734,7 @@
             pltpu.VMEM((height, width), f32),
             pltpu.VMEM((n_col, height, depth), bf16),
             pltpu.VMEM((n_col, depth, BLOCK), bf16),
-            pltpu.VMEM((n_row, n_col, depth, BLOCK), bf16),
+            pltpu.VMEM((n_row // 2 + 1, n_col, depth, 2 * BLOCK), bf16),
             pltpu.VMEM((n_gz, half, BLOCK), f32),
             pltpu.VMEM((n_gz, half, BLOCK), f32),
             pltpu.VMEM((n_gz, half, BLOCK), f32),
@@ -701,8 +760,8 @@
             pltpu.VMEM((BLOCK, BLOCK), f32),
             dma((4,)),
             dma((n_col,)), dma((n_col,)),
-            dma((4,)), dma((4,)),
-            dma((2, len(NATURAL))), dma((n_row, n_col)),
+            dma((6,)), dma((6,)),
+            dma((2, len(NATURAL))), dma((n_row // 2 + 1, 2, n_col)),
             dma((n_gz,)), dma((n_gz,)),
             dma((n_gz,)), dma((n_gz,)),
             dma((2, 2)), dma((2,)),
@@ -719,7 +778,7 @@
             dma((n_gz,)), dma((n_gz,)),
         ],
         compiler_params=pltpu.CompilerParams(
-            collective_id=0, has_side_effects=True, vmem_limit_bytes=63 * 1024 * 1024
+            collective_id=0, has_side_effects=True, vmem_limit_bytes=213 * 256 * 1024
         ),
     )(subtree_lower[0], subtree_upper[0], touched, front.reshape(height, width))
     return (

time: 80.1 us -> 77.1 us (0.963)
  Pallas kernels: 76 us -> 73.6 us
    pallas_call x1, Pallas kernels: 76 us -> 73.6 us  [shards(): pl.pallas_call(functools.partial(front_kernel, n_gz, n_row, n_col), out_s...]
    unnamed x7 -> x5, local copies, waits for them, and re-layouts: 3.06 us -> 2.68 us
where the time goes in v4:
time: 77.1 us; the launch traced here: 77 us
  Pallas kernels  73.6 us (95%)
  local copies, waits for them, and re-layouts  2.68 us (3%)
    pallas_call x1, Pallas kernels, shards(): pl.pallas_call(functools.partial(front_kernel, n_gz, n_row, n_col), out_s...  73.6 us
    unnamed x5, local copies, waits for them, and re-layouts  2.68 us

profile of v4, /device:TPU:144, one launch (start us, length us, event | category | flops | bytes accessed | tf_op | source)
XLA Modules:
  0.0 77.0 jit_solution(17123095900066359224)
XLA Ops:
  0.6 0.0 copy-start
  0.6 0.6 copy-done
  1.3 73.6 %shard_map.67 = (f32[512,128]{1,0:T(8,128)S(1)}, f32[128,128]{1,0:T(8,128)S(1)}, f32[512,128]{1,0:T(8,128)S(1)}) custom-call(bf16[512,512]{1,0:T(8,128)(2,1)} %bitcast.11, bf16[512,512]{1,0:T(8,128)(2,1)} %bitcast.12, s32[1,32]{1,0:T(1,128)S(1)} %copy-done, f32[512,128]{1,0:T(8,128)} %bitcast.13), custom_call_target="tpu_custom_call" | custom-call | tf_op jit(solution)/shard_map/pallas_call | solution.py:721
  74.9 0.7 copy.12
  75.6 0.6 copy.13
  76.3 0.7 copy.14
Async XLA Ops:
  0.6 0.7 copy-start

commit v5 on v4

--- a/solution.py
+++ b/solution.py
@@ -640,6 +640,51 @@
     upper_inverse = finish_elimination(worked, upper_unit)
     panels_out(upper_inverse)
 
+    for copy in sends:
+        copy.wait_send()
+    for step in range(n_gz):
+        j = gz(step)
+        pl.when((j != 0) | (c != 0))(pair_copy(j).wait_send)
+
+    @pl.when(c == 0)
+    def _():
+        for step in range(1, n_gz):
+            column_copy(step).wait_send()
+        for step in range(1, n_col):
+            hand_copy(step).wait_send()
+
+    @pl.when(r < n_row // 2)
+    def _():
+        for at in range(2):
+            chain(1, at).wait_send()
+
+    @pl.when((r == 0) | (r > n_row // 2 + 1))
+    def _():
+        for at in range(2):
+            chain(-1, at).wait_send()
+
+    @pl.when(r == 0)
+    def _():
+        for step in range(1, n_col):
+            pivot_split_copy(step).wait_send()
+        for step in range(1, n_gz):
+            pivot_sum_copy(step).wait_send()
+        for step in range(1, n_row):
+            pivot_row_copy(step).wait_send()
+
+    @pl.when((r == 0) & (g != 0))
+    def _():
+        row_front_copy().wait_send()
+
+    @pl.when(g != r)
+    def _():
+        row_copy().wait_send()
+
+    @pl.when(g == r)
+    def _():
+        for step in range(1, n_row):
+            spread_copy(step).wait_send()
+
     @pl.when((g != 0) | (c != 0))
     def _():
         for step in range(1, n_gz):
@@ -658,55 +703,9 @@
 
         lax.fori_loop(0, panels, add_up, 0)
 
-    for copy in sends:
-        copy.wait_send()
-    for step in range(n_gz):
+    for step in range(1, n_gz):
         j = gz(step)
-
-        @pl.when((j != 0) | (c != 0))
-        def _():
-            pair_copy(j).wait_send()
-            if step:
-                term_copy(j).wait_send()
-
-    @pl.when(c == 0)
-    def _():
-        for step in range(1, n_gz):
-            column_copy(step).wait_send()
-        for step in range(1, n_col):
-            hand_copy(step).wait_send()
-
-    @pl.when(r < n_row // 2)
-    def _():
-        for at in range(2):
-            chain(1, at).wait_send()
-
-    @pl.when((r == 0) | (r > n_row // 2 + 1))
-    def _():
-        for at in range(2):
-            chain(-1, at).wait_send()
-
-    @pl.when(r == 0)
-    def _():
-        for step in range(1, n_col):
-            pivot_split_copy(step).wait_send()
-        for step in range(1, n_gz):
-            pivot_sum_copy(step).wait_send()
-        for step in range(1, n_row):
-            pivot_row_copy(step).wait_send()
-
-    @pl.when((r == 0) & (g != 0))
-    def _():
-        row_front_copy().wait_send()
-
-    @pl.when(g != r)
-    def _():
-        row_copy().wait_send()
-
-    @pl.when(g == r)
-    def _():
-        for step in range(1, n_row):
-            spread_copy(step).wait_send()
+        pl.when((j != 0) | (c != 0))(term_copy(j).wait_send)
 
 
 def shards(n_gz, n_row, n_col, subtree_lower, subtree_upper, touched, front):

time: 77.1 us -> 76.9 us (level)
  no operation moved by 1% of the time
where the time goes in v5:
time: 76.9 us; the launch traced here: 76.8 us
  Pallas kernels  73.5 us (96%)
  local copies, waits for them, and re-layouts  2.68 us (3%)
    pallas_call x1, Pallas kernels, shards(): pl.pallas_call(functools.partial(front_kernel, n_gz, n_row, n_col), out_s...  73.5 us
    unnamed x5, local copies, waits for them, and re-layouts  2.68 us

profile of v5, /device:TPU:144, one launch (start us, length us, event | category | flops | bytes accessed | tf_op | source)
XLA Modules:
  0.0 76.8 jit_solution(16082294625109177167)
XLA Ops:
  0.6 0.0 copy-start
  0.6 0.6 copy-done
  1.3 73.5 %shard_map.67 = (f32[512,128]{1,0:T(8,128)S(1)}, f32[128,128]{1,0:T(8,128)S(1)}, f32[512,128]{1,0:T(8,128)S(1)}) custom-call(bf16[512,512]{1,0:T(8,128)(2,1)} %bitcast.11, bf16[512,512]{1,0:T(8,128)(2,1)} %bitcast.12, s32[1,32]{1,0:T(1,128)S(1)} %copy-done, f32[512,128]{1,0:T(8,128)} %bitcast.13), custom_call_target="tpu_custom_call" | custom-call | tf_op jit(solution)/shard_map/pallas_call | solution.py:720
  74.8 0.7 copy.12
  75.5 0.6 copy.13
  76.1 0.7 copy.14
Async XLA Ops:
  0.6 0.7 copy-start

commit v6 on v5

--- a/solution.py
+++ b/solution.py
@@ -549,6 +549,9 @@
             def _():
                 arrived[x, pl.ds(pl.multiple_of(core * half, half), half), :] = terms[j]
 
+    for slot, step in enumerate(ORDER_OF_K[1:]):
+        mine = gathered.at[0, c, :, side(1)]
+        start(remote(uppers.at[col(step)], mine, up_send.at[slot], up_recv.at[c], col=col(step)))
     @pl.when(r == 0)
     def _():
         for step in range(1, n_col):
@@ -557,9 +560,6 @@
             chain(1, at).start()
             chain(-1, at).start()
 
-    for slot, step in enumerate(ORDER_OF_K[1:]):
-        mine = gathered.at[0, c, :, side(1)]
-        start(remote(uppers.at[col(step)], mine, up_send.at[slot], up_recv.at[c], col=col(step)))
     z_step(0)
     low_start(False)
 

time: 76.9 us -> 76.9 us (level)
  no operation moved by 1% of the time
where the time goes in v6:
time: 76.9 us; the launch traced here: 76.8 us
  Pallas kernels  73.4 us (95%)
  local copies, waits for them, and re-layouts  2.68 us (3%)
    pallas_call x1, Pallas kernels, shards(): pl.pallas_call(functools.partial(front_kernel, n_gz, n_row, n_col), out_s...  73.4 us
    unnamed x5, local copies, waits for them, and re-layouts  2.68 us

profile of v6, /device:TPU:144, one launch (start us, length us, event | category | flops | bytes accessed | tf_op | source)
XLA Modules:
  0.0 76.8 jit_solution(710342939079712550)
XLA Ops:
  0.6 0.0 copy-start
  0.6 0.6 copy-done
  1.3 73.4 %shard_map.67 = (f32[512,128]{1,0:T(8,128)S(1)}, f32[128,128]{1,0:T(8,128)S(1)}, f32[512,128]{1,0:T(8,128)S(1)}) custom-call(bf16[512,512]{1,0:T(8,128)(2,1)} %bitcast.11, bf16[512,512]{1,0:T(8,128)(2,1)} %bitcast.12, s32[1,32]{1,0:T(1,128)S(1)} %copy-done, f32[512,128]{1,0:T(8,128)} %bitcast.13), custom_call_target="tpu_custom_call" | custom-call | tf_op jit(solution)/shard_map/pallas_call | solution.py:720
  74.7 0.7 copy.12
  75.4 0.6 copy.13
  76.1 0.7 copy.14
Async XLA Ops:
  0.6 0.7 copy-start
